TPU v7x, 32 devices: a whole 2x2x4 slice. The times are simulated.
32 devices in a mesh: member: 2 (over core), band: 16 (over z, y, x).
Axes of the slice: x: 2, y: 2, z: 4, core: 2. Of those that a mesh axis runs over, the one named last changes fastest.
Arguments:
- parent_state: float32 [16, 3, 256, 4096], P('member', None, 'band'), parts along dimension 0, may hold values from -6 to 6
- nest_state: float32 [16, 3, 384, 384], P('member', None, 'band'), parts along dimension 0, may hold values from -6 to 6
- offsets: int32 [16, 2], P('member'), parts along dimension 0, may hold values from 2 to 3966, as said below
Outputs:
- parent_out: float32 [16, 3, 256, 4096], P('member', None, 'band'), parts along dimension 0
- nest_out: float32 [16, 3, 384, 384], P('member', None, 'band'), parts along dimension 0
There are 2 independent parts, one for each index of `member`. A program takes and returns all parts, laid end to end along the dimension named above; each array names one. Nothing has to cross between parts.
Inputs may be any that keep to these rules, and one draw needn't show every extreme that they name: Column 0 holds row offsets from 2 to 126, column 1 column offsets from 2 to 3966; in each column some member takes the lowest and some member the highest of its range.
All inputs are finite; a program needn't handle non-finite values.
Results may differ from a plain program's by a relative error of at most 0.00012.
Values sent between devices are 32-bit elements; how exact they have to be, the bound alone decides.
A program may use at most 256 MiB of HBM per device.

v0:
```python
import jax
import jax.numpy as jnp
from jax import lax
from jax.sharding import PartitionSpec as P

NSTEPS = 3


courant = 0.9
friction = 0.02
rotation = 0.05
highest = lax.Precision.HIGHEST


def with_halo(cells, sides, width):
    for axis, dim in sides:
        count = lax.axis_size(axis)
        ends = count - 1
        head = lax.slice_in_dim(cells, 0, width, axis=dim)
        tail = lax.slice_in_dim(cells, cells.shape[dim] - width, cells.shape[dim], axis=dim)
        cells = jnp.concatenate(
            [
                lax.ppermute(tail, axis, [(i, (i + 1) % count) for i in range(ends)]),
                cells,
                lax.ppermute(head, axis, [((i + 1) % count, i) for i in range(ends)]),
            ],
            axis=dim,
        )
    return cells


def interp_matrix(fine, coarse_count):
    rows = jnp.arange(fine, dtype=jnp.int32)[:, None] + 1
    cols = jnp.arange(coarse_count, dtype=jnp.int32)[None, :]
    base = rows // 3
    frac = rows % 3
    upper = frac.astype(jnp.float32) / 3.0
    lower = (3 - frac).astype(jnp.float32) / 3.0
    return jnp.where(cols == base, lower, 0.0) + jnp.where(cols == base + 1, upper, 0.0)


def shift_cols(field):
    return 0.5 * (jnp.roll(field, -1, axis=-1) - jnp.roll(field, 1, axis=-1))


def parent_rows_ext(fields):
    return with_halo(fields, (("band", 2),), 1)


def pad_tile(fields, side_part, ends_part, first_band, last_band):
    extended = with_halo(fields, (("band", 2),), 1)
    top_row = jnp.where(first_band, ends_part[:, :, 0], extended[:, :, 0])
    bottom_row = jnp.where(last_band, ends_part[:, :, 1], extended[:, :, -1])
    rows_full = jnp.concatenate(
        [top_row[:, :, None], extended[:, :, 1:-1], bottom_row[:, :, None]], axis=2
    )
    return jnp.concatenate(
        [side_part[:, :, 0][..., None], rows_full, side_part[:, :, 1][..., None]], axis=3
    )


def nest_step(state, side, ends, first_band, last_band):
    height, zonal, meridional = (state[:, 0], state[:, 1], state[:, 2])
    flows = pad_tile(state[:, 1:3], side[:, 1:3], ends[:, 1:3], first_band, last_band)
    height_new = height - courant * (
        0.5 * (flows[:, 0, 1:-1, 2:] - flows[:, 0, 1:-1, :-2])
        + 0.5 * (flows[:, 1, 2:, 1:-1] - flows[:, 1, :-2, 1:-1])
    )
    padded = pad_tile(height_new[:, None], side[:, 0:1], ends[:, 0:1], first_band, last_band)[:, 0]
    zonal_new = (
        (1.0 - friction) * zonal
        - courant * (0.5 * (padded[:, 1:-1, 2:] - padded[:, 1:-1, :-2]))
        + rotation * meridional
    )
    merid_new = (
        (1.0 - friction) * meridional
        - courant * (0.5 * (padded[:, 2:, 1:-1] - padded[:, :-2, 1:-1]))
        - rotation * zonal
    )
    return jnp.stack([height_new, zonal_new, merid_new], axis=1)


def per_device(parent_state, nest_state, offsets):
    members = parent_state.shape[0]
    band_rows = parent_state.shape[2]
    nest_rows = nest_state.shape[2]
    nest_width = nest_state.shape[3]
    tile_coarse = nest_rows // 3
    span = nest_width // 3
    bands = lax.axis_size("band")
    band_index = lax.axis_index("band")
    first_band = band_index == 0
    last_band = band_index == bands - 1
    rows_off = offsets[:, 0]
    cols_off = offsets[:, 1]
    height, zonal, meridional = (parent_state[:, 0], parent_state[:, 1], parent_state[:, 2])
    flows = parent_rows_ext(parent_state[:, 1:3])
    height_new = height - courant * (shift_cols(zonal) + 0.5 * (flows[:, 1, 2:] - flows[:, 1, :-2]))
    height_ext = parent_rows_ext(height_new[:, None])[:, 0]
    zonal_new = (1.0 - friction) * zonal - courant * shift_cols(height_new) + rotation * meridional
    merid_new = (
        (1.0 - friction) * meridional
        - courant * (0.5 * (height_ext[:, 2:] - height_ext[:, :-2]))
        - rotation * zonal
    )
    stepped = jnp.stack([height_new, zonal_new, merid_new], axis=1)

    def take_pair(field, col0):
        return lax.dynamic_slice_in_dim(field, col0, 2, axis=2)

    near = jax.vmap(take_pair)(stepped, cols_off - 1)
    far = jax.vmap(take_pair)(stepped, cols_off + span - 1)
    west = 2.0 / 3.0 * near[..., 0] + 1.0 / 3.0 * near[..., 1]
    east = 1.0 / 3.0 * far[..., 0] + 2.0 / 3.0 * far[..., 1]
    strip = jnp.stack([west, east], axis=2)
    column_all = lax.all_gather(strip, "band", axis=3, tiled=True)

    def side_window(columns, row0):
        return lax.dynamic_slice_in_dim(
            columns, row0 - 1 + band_index * tile_coarse, tile_coarse + 2, axis=2
        )

    side_rows = jax.vmap(side_window)(column_all, rows_off)
    side = jnp.einsum(
        "ip,mfsp->mfsi", interp_matrix(nest_rows + 2, tile_coarse + 2), side_rows, precision=highest
    )
    global_rows = band_index * band_rows + jnp.arange(band_rows, dtype=jnp.int32)
    row_start = rows_off[:, None]
    top_weight = jnp.where(global_rows[None, :] == row_start - 1, 2.0 / 3.0, 0.0) + jnp.where(
        global_rows[None, :] == row_start, 1.0 / 3.0, 0.0
    )
    bottom_weight = jnp.where(
        global_rows[None, :] == row_start + span - 1, 1.0 / 3.0, 0.0
    ) + jnp.where(global_rows[None, :] == row_start + span, 2.0 / 3.0, 0.0)
    row_weights = jnp.stack([top_weight, bottom_weight], axis=1)
    partial_rows = jnp.einsum("msl,mfln->mfsn", row_weights, stepped, precision=highest)
    ends_full = lax.psum(partial_rows, "band")

    def ends_window(rows_pair, col0):
        return lax.dynamic_slice_in_dim(rows_pair, col0 - 1, span + 2, axis=2)

    ends_cols = jax.vmap(ends_window)(ends_full, cols_off)
    inner_weights = interp_matrix(nest_width + 2, span + 2)[1:-1]
    ends = jnp.einsum("jq,mfsq->mfsj", inner_weights, ends_cols, precision=highest)
    nest = nest_state
    for _ in range(NSTEPS):
        nest = nest_step(nest, side, ends, first_band, last_band)
    coarse = nest.reshape(members, 3, tile_coarse, 3, span, 3).mean(axis=(3, 5))
    whole = lax.all_gather(coarse, "band", axis=2, tiled=True)
    padded_whole = jnp.pad(whole, ((0, 0), (0, 0), (band_rows, band_rows), (0, 0)))

    def band_block(block_rows, row0):
        begin = jnp.clip(band_index * band_rows - row0 + band_rows, 0, span + band_rows)
        return lax.dynamic_slice_in_dim(block_rows, begin, band_rows, axis=1)

    patch = jax.vmap(band_block)(padded_whole, rows_off)
    relative_rows = global_rows[None, :] - rows_off[:, None]
    covered = (relative_rows >= 0) & (relative_rows < span)

    def place(field, block_patch, covered_rows, col0):
        current = lax.dynamic_slice_in_dim(field, col0, span, axis=2)
        merged = jnp.where(covered_rows[None, :, None], block_patch, current)
        return lax.dynamic_update_slice_in_dim(field, merged, col0, axis=2)

    parent_out = jax.vmap(place)(stepped, patch, covered, cols_off)
    return (parent_out, nest)


def solution(mesh):
    in_specs = (P("member", None, "band", None), P("member", None, "band", None), P("member", None))
    out_specs = (P("member", None, "band", None), P("member", None, "band", None))
    return jax.shard_map(
        per_device, mesh=mesh, in_specs=in_specs, out_specs=out_specs, check_vma=False
    )
```

profile of v0, /device:TPU:0, one launch (start us, length us, event | category | flops | bytes accessed | tf_op | source)
XLA Modules:
  0.0 472.9 jit_solution(10395584374216776391)
XLA Ops:
  8.9 5.4 %collective-permute-start.4 = (f32[8,2,1,384]{3,0,2,1:T(8,128)}, f32[8,2,1,384]{3,0,2,1:T(8,128)}, u32[]{:S(2)}, u32[]{:S(2)}) collective-permute-start(f32[8,2,1,384]{3,0,2,1:T(8,128)} %copy.351), channel_id=1, source_target_pairs={{0,1},{1,2},{2,3},{3,4},{4,5},{5,6},{6,7},{7,8},{8,9},{9,10},{10,1... | collective-permute-start | bytes 73736 | tf_op jit(solution)/shard_map/ppermute | solution.py:23
  16.2 2.6 fusion.100
  19.0 4.6 collective-permute-start.1
  26.9 1.7 slice_bitcast_fusion.2
  28.7 3.6 fusion.102
  34.3 2.2 slice-done.2
  36.4 2.4 copy.344
  42.2 3.0 fusion.9
  47.5 6.7 %fusion.13 = (f32[8,1,16,4096]{3,2,1,0:T(8,128)}, f32[8,1,16,4096]{3,2,0,1:T(8,128)S(1)}) fusion(f32[8,1,16,1]{3,2,0,1:T(8,128)S(1)} %get-tuple-element.67, f32[8,1,16,4095]{3,2,0,1:T(8,128)S(1)} %get-tuple-element.69, f32[8,1,16,4095]{3,2,0,1:T(8,128)S(1)} %get-tuple-element.68, f32[8,1,16,1]{3,2,0,1:T(8,128)S(1)} %get-tuple-element.66, ...), kind=kLoop, calls=%fused_computation.34 | loop fusion | flops 7864320 | bytes 23068672 | tf_op jit(solution)/shard_map/add | solution.py:100
  56.6 5.4 %collective-permute-start.2 = (f32[8,1,1,4096]{3,0,2,1:T(8,128)S(1)}, f32[8,1,1,4096]{3,0,2,1:T(8,128)S(1)}, u32[]{:S(2)}, u32[]{:S(2)}) collective-permute-start(f32[8,1,1,4096]{3,0,2,1:T(8,128)S(1)} %copy.284), channel_id=1, source_target_pairs={{0,1},{1,2},{2,3},{3,4},{4,5},{5,6},{6,7},{7,8},{8,9},{9,10},{10,1... | collective-permute-start | bytes 393224 | tf_op jit(solution)/shard_map/ppermute | solution.py:23
  67.2 3.1 fusion.3
  70.3 3.1 pad_maximum_fusion
  73.5 4.4 convolution_bitcast_fusion
  77.9 48.6 %copy.296 = f32[8,3,16,4096]{2,1,0,3:T(4,128)} copy(f32[8,3,16,4096]{3,2,1,0:T(8,128)} %pad_maximum_fusion) | data formatting | bytes 12582912 | tf_op jit(solution)/shard_map/stack | solution.py:106
  127.8 1.3 gather_fusion.1
  129.3 47.1 %all_gather.6 = f32[8,3,2,256]{0,2,1,3:T(2,128)S(1)} all-gather(f32[8,3,2,16]{0,2,1,3:T(2,128)S(1)} %copy.304), channel_id=1, replica_groups=mesh['member'=2,'band'=16] {'band'}, dimensions={3}, use_global_device_ids=true | all-gather | bytes 52224 | tf_op jit(solution)/shard_map/all_gather | solution.py:116
  176.4 4.1 copy.305
  180.5 2.3 gather_fusion.3
  183.6 8.1 %all-reduce.7.cloned.1.call-done = f32[8,3,2,4096]{3,2,1,0:T(2,128)} async-done(((f32[8,3,2,4096]{3,2,1,0:T(2,128)}), f32[8,3,2,4096]{3,2,1,0:T(2,128)}) %all-reduce.7.cloned.1.call-update) | async-done | bytes 786448 | tf_op jit(solution)/shard_map/psum | solution.py:137
  191.8 36.1 %copy.291 = f32[8,3,2,4096]{1,2,0,3:T(2,128)} copy(f32[8,3,2,4096]{3,2,1,0:T(2,128)} %all-reduce.7.cloned.1.call-done) | data formatting | bytes 1572864 | tf_op jit(solution)/shard_map/psum | solution.py:137
  227.9 3.9 gather_fusion
  231.8 2.0 copy.292
  235.1 3.4 collective-permute-start.6
  240.1 4.0 collective-permute-done.7
  245.9 4.7 collective-permute-start.8
  250.7 1.5 collective-permute-done.8
  252.4 4.8 %collective-permute-start.10 = (f32[8,1,1,384]{3,0,2,1:T(8,128)S(1)}, f32[8,1,1,384]{3,0,2,1:T(8,128)S(1)}, u32[]{:S(2)}, u32[]{:S(2)}) collective-permute-start(f32[8,1,1,384]{3,0,2,1:T(8,128)S(1)} %get-tuple-element.97), channel_id=1, source_target_pairs={{0,1},{1,2},{2,3},{3,4},{4,5},{5,6},{6,7},{7,8},{8,9},{9,10},{10,1... | collective-permute-start | bytes 36872 | tf_op jit(solution)/shard_map/ppermute | solution.py:23
  258.7 5.4 %collective-permute-done.11 = f32[8,1,1,384]{3,0,2,1:T(8,128)S(1)} collective-permute-done((f32[8,1,1,384]{3,0,2,1:T(8,128)S(1)}, f32[8,1,1,384]{3,0,2,1:T(8,128)S(1)}, u32[]{:S(2)}, u32[]{:S(2)}) %collective-permute-start.11) | collective-permute-done | bytes 12320 | tf_op jit(solution)/shard_map/ppermute | solution.py:25
  265.9 5.4 %collective-permute-start.12 = (f32[8,2,1,384]{3,0,2,1:T(8,128)S(1)}, f32[8,2,1,384]{3,0,2,1:T(8,128)S(1)}, u32[]{:S(2)}, u32[]{:S(2)}) collective-permute-start(f32[8,2,1,384]{3,0,2,1:T(8,128)S(1)} %get-tuple-element.92), channel_id=1, source_target_pairs={{0,1},{1,2},{2,3},{3,4},{4,5},{5,6},{6,7},{7,8},{8,9},{9,10},{10,1... | collective-permute-start | bytes 73736 | tf_op jit(solution)/shard_map/ppermute | solution.py:23
  271.4 1.5 collective-permute-done.12
  273.1 4.8 %collective-permute-start.14 = (f32[8,1,1,384]{3,0,2,1:T(8,128)S(1)}, f32[8,1,1,384]{3,0,2,1:T(8,128)S(1)}, u32[]{:S(2)}, u32[]{:S(2)}) collective-permute-start(f32[8,1,1,384]{3,0,2,1:T(8,128)S(1)} %get-tuple-element.95), channel_id=1, source_target_pairs={{0,1},{1,2},{2,3},{3,4},{4,5},{5,6},{6,7},{7,8},{8,9},{9,10},{10,1... | collective-permute-start | bytes 36872 | tf_op jit(solution)/shard_map/ppermute | solution.py:23
  278.0 1.5 collective-permute-start.15
  279.5 7.2 %copy.319 = f32[8,1,24,384]{0,1,3,2:T(1,128)} copy(f32[8,1,24,384]{3,0,2,1:T(8,128)S(1)} %fusion.29) | data formatting | bytes 589824 | tf_op jit(solution)/shard_map/sub | solution.py:65
  287.2 2.9 copy.340
  290.1 2.9 copy.341
  293.1 24.1 %maximum_reduce_fusion = f32[8,3,8,128]{0,1,3,2:T(4,128)S(1)} fusion(f32[8,1,8,3,128,3]{0,1,5,4,3,2:T(1,128)} %bitcast.156, f32[8,1,8,3,128,3]{0,1,5,4,3,2:T(1,128)} %bitcast.155, f32[8,1,8,3,128,3]{0,1,5,4,3,2:T(1,128)} %bitcast.154), kind=kLoop, calls=%fused_computation.9 | loop fusion | flops 638976 | bytes 983040 | tf_op jit(solution)/shard_map/reduce_sum | solution.py:148
  318.6 3.2 gather_fusion.5
  323.8 60.8 %all-gather.2.cloned.1.call-done = f32[8,3,128,128]{3,0,1,2:T(8,128)} async-done(((f32[8,3,8,128]{3,0,1,2:T(8,128)}), f32[8,3,128,128]{3,0,1,2:T(8,128)}) %all-gather.2.cloned.1.call-update) | async-done | bytes 1572880 | tf_op jit(solution)/shard_map/all_gather | solution.py:149
  384.6 2.0 copy.328
  388.2 77.9 %while.1 = (s32[]{:T(128)}, f32[8,3,16,4096]{3,2,1,0:T(8,128)}, s32[8,4]{0,1:T(4,128)S(1)}, f32[8,3,16,128]{3,2,1,0:T(8,128)S(1)}, s32[]{:T(128)}, /*index=5*/s32[4]{0:T(128)S(1)}, s32[]{:T(128)}) while((s32[]{:T(128)}, f32[8,3,16,4096]{3,2,1,0:T(8,128)}, s32[8,4]{0,1:T(4,128)S(1)}, f32[8,3,16,128]{3,2,1,0:T(8,128)S(1)}, s32[]{:T(128)}, ...), condition=%wide.while_cond, body=%wide.while_body.sunk | while | flops 6173 | bytes 123083 | solution.py:163
  388.9 3.2 and_reduce_fusion.2
  392.1 2.8 dynamic-slice_select_fusion.2
  394.9 3.1 dynamic-update-slice.3
  398.6 3.2 and_reduce_fusion.2
  401.8 2.8 dynamic-slice_select_fusion.2
  404.6 3.1 dynamic-update-slice.3
  408.4 3.2 and_reduce_fusion.2
  411.6 2.8 dynamic-slice_select_fusion.2
  414.4 3.1 dynamic-update-slice.3
  418.1 3.2 and_reduce_fusion.2
  421.3 2.8 dynamic-slice_select_fusion.2
  424.1 3.1 dynamic-update-slice.3
  427.8 3.2 and_reduce_fusion.2
  431.0 2.8 dynamic-slice_select_fusion.2
  433.8 3.1 dynamic-update-slice.3
  437.6 3.2 and_reduce_fusion.2
  440.8 2.8 dynamic-slice_select_fusion.2
  443.6 3.1 dynamic-update-slice.3
  447.3 3.2 and_reduce_fusion.2
  450.5 2.8 dynamic-slice_select_fusion.2
  453.3 3.1 dynamic-update-slice.3
  457.0 3.2 and_reduce_fusion.2
  460.2 2.8 dynamic-slice_select_fusion.2
  463.0 3.1 dynamic-update-slice.3
  (186 shorter events, 43.5 us)
Async XLA Ops:
  7.2 184.6 %all-reduce.7.cloned.1.call-start = ((), (), s32[]{:S(2)}) async-start(), calls=%async_computation | async-start | bytes 1572864 | tf_op jit(solution)/shard_map/psum | solution.py:137
  8.9 225.2 %collective-permute-start.4 = (f32[8,2,1,384]{3,0,2,1:T(8,128)}, f32[8,2,1,384]{3,0,2,1:T(8,128)}, u32[]{:S(2)}, u32[]{:S(2)}) collective-permute-start(f32[8,2,1,384]{3,0,2,1:T(8,128)} %copy.351), channel_id=1, source_target_pairs={{0,1},{1,2},{2,3},{3,4},{4,5},{5,6},{6,7},{7,8},{8,9},{9,10},{10,1... | collective-permute-start | bytes 73736 | tf_op jit(solution)/shard_map/ppermute | solution.py:23
  14.9 219.1 %collective-permute-start.5 = (f32[8,2,1,384]{3,0,2,1:T(8,128)}, f32[8,2,1,384]{3,0,2,1:T(8,128)}, u32[]{:S(2)}, u32[]{:S(2)}) collective-permute-start(f32[8,2,1,384]{3,0,2,1:T(8,128)} %copy.353), channel_id=1, source_target_pairs={{1,0},{2,1},{3,2},{4,3},{5,4},{6,5},{7,6},{8,7},{9,8},{10,9},{11,1... | collective-permute-start | bytes 73736 | tf_op jit(solution)/shard_map/ppermute | solution.py:25
  19.0 20.8 %collective-permute-start.1 = (f32[8,2,1,4096]{3,0,2,1:T(8,128)S(1)}, f32[8,2,1,4096]{3,0,2,1:T(8,128)S(1)}, u32[]{:S(2)}, u32[]{:S(2)}) collective-permute-start(f32[8,2,1,4096]{3,0,2,1:T(8,128)S(1)} %copy.347), channel_id=1, source_target_pairs={{0,1},{1,2},{2,3},{3,4},{4,5},{5,6},{6,7},{7,8},{8,9},{9,10},{10,1... | collective-permute-start | bytes 786440 | tf_op jit(solution)/shard_map/ppermute | solution.py:23
  23.8 16.1 %collective-permute-start = (f32[8,2,1,4096]{3,0,2,1:T(8,128)S(1)}, f32[8,2,1,4096]{3,0,2,1:T(8,128)S(1)}, u32[]{:S(2)}, u32[]{:S(2)}) collective-permute-start(f32[8,2,1,4096]{3,0,2,1:T(8,128)S(1)} %copy.345), channel_id=1, source_target_pairs={{1,0},{2,1},{3,2},{4,3},{5,4},{6,5},{7,6},{8,7},{9,8},{10,9},{11,1... | collective-permute-start | bytes 786440 | tf_op jit(solution)/shard_map/ppermute | solution.py:25
  28.7 3.7 copy-start.26
  32.3 1.9 copy-start.23
  33.0 1.3 copy-start.15
  34.3 2.2 slice-start.2
  36.4 2.4 copy-start.4
  36.4 3.9 slice-start
  38.9 2.5 slice-start.1
  39.8 2.4 copy-start.3
  45.3 1.6 copy-start
  45.3 2.2 copy-start.1
  54.3 8.3 %copy-start.13 = (s32[386]{0:T(512)S(1)}, s32[386]{0:T(512)}, u32[]{:S(2)}) copy-start(s32[386]{0:T(512)} %broadcast_add_fusion) | copy-start | bytes 4636
  54.3 9.0 %copy-start.12 = (f32[386]{0:T(512)S(1)}, f32[386]{0:T(512)}, u32[]{:S(2)}) copy-start(f32[386]{0:T(512)} %convert_multiply_fusion.1) | copy-start | bytes 4636
  54.3 9.7 %copy-start.11 = (f32[386]{0:T(512)S(1)}, f32[386]{0:T(512)}, u32[]{:S(2)}) copy-start(f32[386]{0:T(512)} %convert_multiply_fusion) | copy-start | bytes 4636
  54.3 10.3 %copy-start.14 = (s32[386]{0:T(512)S(1)}, s32[386]{0:T(512)}, u32[]{:S(2)}) copy-start(s32[386]{0:T(512)} %add_select_fusion.1) | copy-start | bytes 4636
  55.3 10.2 %collective-permute-start.3 = (f32[8,1,1,4096]{3,0,2,1:T(8,128)}, f32[8,1,1,4096]{3,0,2,1:T(8,128)}, u32[]{:S(2)}, u32[]{:S(2)}) collective-permute-start(f32[8,1,1,4096]{3,0,2,1:T(8,128)} %copy.285), channel_id=1, source_target_pairs={{1,0},{2,1},{3,2},{4,3},{5,4},{6,5},{7,6},{8,7},{9,8},{10,9},{11,1... | collective-permute-start | bytes 393224 | tf_op jit(solution)/shard_map/ppermute | solution.py:25
  56.6 9.9 %collective-permute-start.2 = (f32[8,1,1,4096]{3,0,2,1:T(8,128)S(1)}, f32[8,1,1,4096]{3,0,2,1:T(8,128)S(1)}, u32[]{:S(2)}, u32[]{:S(2)}) collective-permute-start(f32[8,1,1,4096]{3,0,2,1:T(8,128)S(1)} %copy.284), channel_id=1, source_target_pairs={{0,1},{1,2},{2,3},{3,4},{4,5},{5,6},{6,7},{7,8},{8,9},{9,10},{10,1... | collective-permute-start | bytes 393224 | tf_op jit(solution)/shard_map/ppermute | solution.py:23
  67.2 3.1 copy-start.2
  70.3 3.1 copy-start.17
  70.3 3.1 copy-start.18
  77.9 306.7 %all-gather.2.cloned.1.call-start = ((), (), s32[]{:S(2)}) async-start(), calls=%async_computation.1 | async-start | bytes 1671168 | tf_op jit(solution)/shard_map/all_gather | solution.py:149
  129.1 51.4 %copy-start.9 = (s32[8]{0:T(128)S(1)}, s32[8]{0:T(128)}, u32[]{:S(2)}) copy-start(s32[8]{0:T(128)} %get-tuple-element.126) | copy-start | bytes 100
  129.1 53.9 %copy-start.27 = (f32[26]{0:T(128)S(1)}, f32[26]{0:T(128)}, u32[]{:S(2)}) copy-start(f32[26]{0:T(128)} %get-tuple-element.136) | copy-start | bytes 316
  129.1 53.9 %copy-start.28 = (f32[26]{0:T(128)S(1)}, f32[26]{0:T(128)}, u32[]{:S(2)}) copy-start(f32[26]{0:T(128)} %get-tuple-element.137) | copy-start | bytes 316
  183.6 44.3 %copy-start.8 = (s32[8]{0:T(128)S(1)}, s32[8]{0:T(128)}, u32[]{:S(2)}) copy-start(s32[8]{0:T(128)} %get-tuple-element.122) | copy-start | bytes 100
  183.6 50.1 %copy-start.19 = (s32[384]{0:T(512)S(1)}, s32[384]{0:T(512)}, u32[]{:S(2)}) copy-start(s32[384]{0:T(512)} %slice.432) | copy-start | bytes 4612
  183.6 50.1 %copy-start.20 = (f32[384]{0:T(512)S(1)}, f32[384]{0:T(512)}, u32[]{:S(2)}) copy-start(f32[384]{0:T(512)} %slice.433) | copy-start | bytes 4612
  183.6 50.1 %copy-start.21 = (f32[384]{0:T(512)S(1)}, f32[384]{0:T(512)}, u32[]{:S(2)}) copy-start(f32[384]{0:T(512)} %slice.434) | copy-start | bytes 4612
  183.6 50.1 %copy-start.22 = (s32[384]{0:T(512)S(1)}, s32[384]{0:T(512)}, u32[]{:S(2)}) copy-start(s32[384]{0:T(512)} %slice.431) | copy-start | bytes 4612
  183.6 51.2 %copy-start.7 = (f32[8,1,24,384]{3,2,1,0:T(8,128)S(1)}, f32[8,1,24,384]{3,2,1,0:T(8,128)}, u32[]{:S(2)}) copy-start(f32[8,1,24,384]{3,2,1,0:T(8,128)} %get-tuple-element.87) | copy-start | bytes 884740
  231.8 12.6 %copy-start.5 = (f32[8,1,24,384]{3,2,1,0:T(8,128)S(1)}, f32[8,1,24,384]{3,2,1,0:T(8,128)}, u32[]{:S(2)}) copy-start(f32[8,1,24,384]{3,2,1,0:T(8,128)} %get-tuple-element.86) | copy-start | bytes 884740
  231.8 12.6 %copy-start.6 = (f32[8,1,24,384]{3,2,1,0:T(8,128)S(1)}, f32[8,1,24,384]{3,2,1,0:T(8,128)}, u32[]{:S(2)}) copy-start(f32[8,1,24,384]{3,2,1,0:T(8,128)} %get-tuple-element.88) | copy-start | bytes 884740
  235.1 5.0 %collective-permute-start.6 = (f32[8,1,1,384]{3,0,2,1:T(8,128)S(1)}, f32[8,1,1,384]{3,0,2,1:T(8,128)S(1)}, u32[]{:S(2)}, u32[]{:S(2)}) collective-permute-start(f32[8,1,1,384]{3,0,2,1:T(8,128)S(1)} %get-tuple-element.99), channel_id=1, source_target_pairs={{0,1},{1,2},{2,3},{3,4},{4,5},{5,6},{6,7},{7,8},{8,9},{9,10},{10,1... | collective-permute-start | bytes 36872 | tf_op jit(solution)/shard_map/ppermute | solution.py:23
  238.5 5.6 %collective-permute-start.7 = (f32[8,1,1,384]{3,0,2,1:T(8,128)S(1)}, f32[8,1,1,384]{3,0,2,1:T(8,128)S(1)}, u32[]{:S(2)}, u32[]{:S(2)}) collective-permute-start(f32[8,1,1,384]{3,0,2,1:T(8,128)S(1)} %get-tuple-element.100), channel_id=1, source_target_pairs={{1,0},{2,1},{3,2},{4,3},{5,4},{6,5},{7,6},{8,7},{9,8},{10,9},{11,1... | collective-permute-start | bytes 36872 | tf_op jit(solution)/shard_map/ppermute | solution.py:25
  244.6 6.0 %collective-permute-start.9 = (f32[8,2,1,384]{3,0,2,1:T(8,128)S(1)}, f32[8,2,1,384]{3,0,2,1:T(8,128)S(1)}, u32[]{:S(2)}, u32[]{:S(2)}) collective-permute-start(f32[8,2,1,384]{3,0,2,1:T(8,128)S(1)} %get-tuple-element.93), channel_id=1, source_target_pairs={{1,0},{2,1},{3,2},{4,3},{5,4},{6,5},{7,6},{8,7},{9,8},{10,9},{11,1... | collective-permute-start | bytes 73736 | tf_op jit(solution)/shard_map/ppermute | solution.py:25
  245.9 6.2 %collective-permute-start.8 = (f32[8,2,1,384]{3,0,2,1:T(8,128)S(1)}, f32[8,2,1,384]{3,0,2,1:T(8,128)S(1)}, u32[]{:S(2)}, u32[]{:S(2)}) collective-permute-start(f32[8,2,1,384]{3,0,2,1:T(8,128)S(1)} %get-tuple-element.94), channel_id=1, source_target_pairs={{0,1},{1,2},{2,3},{3,4},{4,5},{5,6},{6,7},{7,8},{8,9},{9,10},{10,1... | collective-permute-start | bytes 73736 | tf_op jit(solution)/shard_map/ppermute | solution.py:23
  252.4 6.2 %collective-permute-start.10 = (f32[8,1,1,384]{3,0,2,1:T(8,128)S(1)}, f32[8,1,1,384]{3,0,2,1:T(8,128)S(1)}, u32[]{:S(2)}, u32[]{:S(2)}) collective-permute-start(f32[8,1,1,384]{3,0,2,1:T(8,128)S(1)} %get-tuple-element.97), channel_id=1, source_target_pairs={{0,1},{1,2},{2,3},{3,4},{4,5},{5,6},{6,7},{7,8},{8,9},{9,10},{10,1... | collective-permute-start | bytes 36872 | tf_op jit(solution)/shard_map/ppermute | solution.py:23
  257.3 6.8 %collective-permute-start.11 = (f32[8,1,1,384]{3,0,2,1:T(8,128)S(1)}, f32[8,1,1,384]{3,0,2,1:T(8,128)S(1)}, u32[]{:S(2)}, u32[]{:S(2)}) collective-permute-start(f32[8,1,1,384]{3,0,2,1:T(8,128)S(1)} %get-tuple-element.98), channel_id=1, source_target_pairs={{1,0},{2,1},{3,2},{4,3},{5,4},{6,5},{7,6},{8,7},{9,8},{10,9},{11,1... | collective-permute-start | bytes 36872 | tf_op jit(solution)/shard_map/ppermute | solution.py:25
  264.6 6.8 %collective-permute-start.13 = (f32[8,2,1,384]{3,0,2,1:T(8,128)S(1)}, f32[8,2,1,384]{3,0,2,1:T(8,128)S(1)}, u32[]{:S(2)}, u32[]{:S(2)}) collective-permute-start(f32[8,2,1,384]{3,0,2,1:T(8,128)S(1)} %get-tuple-element.91), channel_id=1, source_target_pairs={{1,0},{2,1},{3,2},{4,3},{5,4},{6,5},{7,6},{8,7},{9,8},{10,9},{11,1... | collective-permute-start | bytes 73736 | tf_op jit(solution)/shard_map/ppermute | solution.py:25
  265.9 7.0 %collective-permute-start.12 = (f32[8,2,1,384]{3,0,2,1:T(8,128)S(1)}, f32[8,2,1,384]{3,0,2,1:T(8,128)S(1)}, u32[]{:S(2)}, u32[]{:S(2)}) collective-permute-start(f32[8,2,1,384]{3,0,2,1:T(8,128)S(1)} %get-tuple-element.92), channel_id=1, source_target_pairs={{0,1},{1,2},{2,3},{3,4},{4,5},{5,6},{6,7},{7,8},{8,9},{9,10},{10,1... | collective-permute-start | bytes 73736 | tf_op jit(solution)/shard_map/ppermute | solution.py:23
  273.1 13.6 %collective-permute-start.14 = (f32[8,1,1,384]{3,0,2,1:T(8,128)S(1)}, f32[8,1,1,384]{3,0,2,1:T(8,128)S(1)}, u32[]{:S(2)}, u32[]{:S(2)}) collective-permute-start(f32[8,1,1,384]{3,0,2,1:T(8,128)S(1)} %get-tuple-element.95), channel_id=1, source_target_pairs={{0,1},{1,2},{2,3},{3,4},{4,5},{5,6},{6,7},{7,8},{8,9},{9,10},{10,1... | collective-permute-start | bytes 36872 | tf_op jit(solution)/shard_map/ppermute | solution.py:23
  278.0 8.7 %collective-permute-start.15 = (f32[8,1,1,384]{3,0,2,1:T(8,128)S(1)}, f32[8,1,1,384]{3,0,2,1:T(8,128)S(1)}, u32[]{:S(2)}, u32[]{:S(2)}) collective-permute-start(f32[8,1,1,384]{3,0,2,1:T(8,128)S(1)} %get-tuple-element.96), channel_id=1, source_target_pairs={{1,0},{2,1},{3,2},{4,3},{5,4},{6,5},{7,6},{8,7},{9,8},{10,9},{11,1... | collective-permute-start | bytes 36872 | tf_op jit(solution)/shard_map/ppermute | solution.py:25
  317.2 1.2 copy-start.25
  317.2 1.2 copy-start.29
  317.2 1.3 copy-start.16
  317.2 1.3 copy-start.24
  386.6 1.6 copy-start.10
Sparse Core Ops, SparseCore 0:
  78.0 113.7 all-reduce.6
  318.5 66.0 all-gather.1
where the time goes:
time: 480 us; the launch traced here: 473 us
  local copies, waits for them, and re-layouts  179 us (37%)
  other arithmetic  96.7 us (20%)
  waiting for transfers between devices  81.5 us (17%)
  starting transfers between devices  49.2 us (10%)
  blocking collectives  47.1 us (10%)
  between operations  14.9 us (3%)
  matrix products  4.82 us (1%)
    all_gather x1, waiting for transfers between devices, per_device(): whole = lax.all_gather(coarse, 'band', axis=2, tiled=True)  60.8 us
    another operation x1, local copies, waits for them, and re-layouts, per_device(): stepped = jnp.stack([height_new, zonal_new, merid_new], axis=1)  48.6 us
    scatter x16, other arithmetic  47.9 us
    all_gather x1, blocking collectives, per_device(): column_all = lax.all_gather(strip, 'band', axis=3, tiled=True)  47.1 us
    ppermute x8, starting transfers between devices, with_halo(): lax.ppermute(tail, axis, [(i, (i + 1) % count) for i in range(ends)])  38.5 us
    psum x1, local copies, waits for them, and re-layouts, per_device(): ends_full = lax.psum(partial_rows, 'band')  36.1 us
    scatter x24, local copies, waits for them, and re-layouts  29.9 us
    reduce_sum x1, other arithmetic, per_device(): coarse = nest.reshape(members, 3, tile_coarse, 3, span, 3).mean(axis=(3, 5))  24.1 us
  transfers between devices with their start and end apart: 18, of which 7 were waited for; matrix products, arithmetic and copies ran while one was open for 33% of the time, Pallas kernels for 0%

commit v1 on v0

v1 whole, which is shorter than its diff:
```python
import functools

import jax
import jax.numpy as jnp
from jax import lax
from jax.experimental import pallas as pl
from jax.experimental.pallas import tpu as pltpu
from jax.sharding import PartitionSpec as P

NSTEPS = 3
MESH = pl.DeviceIdType.MESH

courant = 0.9
friction = 0.02
rotation = 0.05
half = 0.5 * courant
keep = 1.0 - friction
highest = lax.Precision.HIGHEST
LANES = 128
HALO = 8


def lane_roll(x, shift):
    size = x.shape[-1]
    return pltpu.roll(x, shift % size, x.ndim - 1)


def row_roll(x, shift):
    size = x.shape[-2]
    return pltpu.roll(x, shift % size, x.ndim - 2)


def dx(x):
    return 0.5 * (lane_roll(x, -1) - lane_roll(x, 1))


def iota(shape, dim):
    return lax.broadcasted_iota(jnp.int32, shape, dim)


def gather_kernel(span, bands, off_ref, band_ref, par_ref, edge_ref, strip_ref, ends_ref):
    mem = pl.program_id(0)
    rows, width = par_ref.shape[2], par_ref.shape[3]
    row0, col0 = off_ref[mem, 0], off_ref[mem, 1]
    band = band_ref[0]

    z_top, z_bot = par_ref[0, 1, 0:1, :], par_ref[0, 1, rows - 1 : rows, :]
    m_top, m_bot = par_ref[0, 2, 0:1, :], par_ref[0, 2, rows - 1 : rows, :]
    edge_ref[0, 0, 0:1, :] = m_top
    edge_ref[0, 0, 1:2, :] = par_ref[0, 0, 0:1, :] - courant * dx(z_top) - half * par_ref[0, 2, 1:2, :]
    edge_ref[1, 0, 0:1, :] = m_bot
    edge_ref[1, 0, 1:2, :] = (
        par_ref[0, 0, rows - 1 : rows, :] - courant * dx(z_bot) + half * par_ref[0, 2, rows - 2 : rows - 1, :]
    )

    blocks = width // LANES
    count = span // LANES + 2
    first = lax.rem(col0 - 4 + width, width)
    block0 = first // LANES
    shift = first - block0 * LANES
    parts = [
        par_ref[0, :, :, pl.ds(pl.multiple_of(lax.rem(block0 + k, blocks) * LANES, LANES), LANES)]
        for k in range(count)
    ]
    wide = jnp.concatenate(parts, axis=-1).reshape(3 * rows, count * LANES)
    wide = pltpu.roll(wide, lax.rem(count * LANES - shift, count * LANES), 1)
    wide = wide[:, : span + LANES].reshape(3, rows, span + LANES)
    h, z, m = wide[0], wide[1], wide[2]
    a = h - courant * dx(z)
    b = keep * z - courant * dx(a) + rotation * m
    cc = keep * m - rotation * z
    shape = h.shape
    lane = iota(shape, 1)
    west = jnp.where(lane == 3, 2.0 / 3.0, 0.0) + jnp.where(lane == 4, 1.0 / 3.0, 0.0)
    east = jnp.where(lane == span + 3, 1.0 / 3.0, 0.0) + jnp.where(lane == span + 4, 2.0 / 3.0, 0.0)
    slot = iota((rows, LANES), 1)
    total = jnp.zeros((rows, LANES), jnp.float32)
    for q, field in enumerate((a, m, b, dx(m), cc)):
        for s, weight in enumerate((west, east)):
            value = jnp.sum(field * weight, axis=1, keepdims=True)
            total = total + jnp.where(slot == q * 16 + s + 2 * mem, value, 0.0)

    @pl.when(mem == 0)
    def _():
        strip_ref[...] = jnp.zeros_like(strip_ref)

    strip_ref[...] += total

    row = iota(shape, 0) + band * rows
    for end in range(2):
        near = row0 - 1 if end == 0 else row0 + span - 1
        lo, hi = (2.0 / 3.0, 1.0 / 3.0) if end == 0 else (1.0 / 3.0, 2.0 / 3.0)

        def w(i):
            return jnp.where(i == near, lo, 0.0) + jnp.where(i == near + 1, hi, 0.0)

        def u(i):
            return -half * (w(i - 1) - w(i + 1))

        wr, ur = w(row), u(row)
        vr = -half * (u(row - 1) - u(row + 1))
        h1 = jnp.sum(wr * a + ur * m, axis=0, keepdims=True)
        z1 = jnp.sum(wr * (keep * z + rotation * m), axis=0, keepdims=True) - courant * dx(h1)
        m1 = jnp.sum(wr * cc + ur * a + vr * m, axis=0, keepdims=True)
        for f, value in enumerate((h1, z1, m1)):
            ends_ref[end, f, pl.ds(mem, 1), :] = value


def nest_kernel(
    bands,
    span,
    off_ref,
    nest_ref,
    edge_ref,
    strip_ref,
    ends_ref,
    nest_out,
    patch,
    halo,
    ext,
    strips,
    endbuf,
    ghost,
    acc,
    coarse,
    dealt,
    cbuf,
    sbuf,
    nest_send,
    nest_recv,
    edge_send,
    edge_recv,
    strip_send,
    strip_recv,
    end_send,
    end_recv,
    mid_send,
    mid_recv,
    out_send,
    out_recv,
    local_sem,
):
    me = lax.axis_index("band")
    group = lax.axis_index("member")
    members, _, nrows, nwidth = nest_ref.shape
    prows = strip_ref.shape[0]
    tile = nrows // 3
    per = bands // members
    top_senders = bands // 2 + 1

    def remote(src, dst, send, recv, to):
        return pltpu.make_async_remote_copy(
            src_ref=src, dst_ref=dst, send_sem=send, recv_sem=recv, device_id=(group, to), device_id_type=MESH
        )

    barrier = pltpu.get_barrier_semaphore()

    def greet(j, _):
        pl.semaphore_signal(barrier, inc=1, device_id=(group, lax.rem(me + j, bands)), device_id_type=MESH)
        return 0

    lax.fori_loop(1, bands, greet, 0)
    own = pltpu.make_async_copy(nest_ref, ext.at[:, :, pl.ds(HALO, nrows), :], local_sem)
    own.start()
    pl.semaphore_wait(barrier, bands - 1)

    def nest_down(to):
        return remote(
            nest_ref.at[:, :, pl.ds(nrows - HALO, HALO), :], ext.at[:, :, pl.ds(0, HALO), :], nest_send.at[0], nest_recv.at[0], to
        )

    def nest_up(to):
        return remote(
            nest_ref.at[:, :, pl.ds(0, HALO), :],
            ext.at[:, :, pl.ds(HALO + nrows, HALO), :],
            nest_send.at[1],
            nest_recv.at[1],
            to,
        )

    def edge_down(to):
        return remote(edge_ref.at[1], halo.at[0], edge_send.at[0], edge_recv.at[0], to)

    def edge_up(to):
        return remote(edge_ref.at[0], halo.at[1], edge_send.at[1], edge_recv.at[1], to)

    def strip_copy(slot, to, index):
        return remote(strip_ref, strips.at[pl.ds(pl.multiple_of((slot + 1) * prows, prows), prows), :], strip_send.at[index], strip_recv.at[slot], to)

    def end_copy(end, slot, to):
        return remote(ends_ref.at[end], endbuf.at[slot], end_send.at[end], end_recv.at[slot], to)

    first, last = me == 0, me == bands - 1

    @pl.when(jnp.logical_not(first))
    def _():
        nest_up(me - 1).start()

    @pl.when(jnp.logical_not(last))
    def _():
        nest_down(me + 1).start()

    def send_strip(j, _):
        strip_copy(me, lax.rem(me + j, bands), j).start()
        return 0

    lax.fori_loop(1, bands, send_strip, 0)

    sends_top = jnp.logical_and(me > 0, me < top_senders)
    sends_bottom = jnp.logical_and(me < bands - 1, me >= bands - top_senders)

    @pl.when(sends_top)
    def _():
        end_copy(0, me, 0).start()

    @pl.when(sends_bottom)
    def _():
        end_copy(1, bands - 1 - me, bands - 1).start()

    @pl.when(jnp.logical_not(first))
    def _():
        edge_up(me - 1).start()

    @pl.when(jnp.logical_not(last))
    def _():
        edge_down(me + 1).start()

    pad = strips.shape[0] - (bands + 1) * prows
    strips[pl.ds(0, prows), :] = jnp.zeros((prows, LANES), jnp.float32)
    strips[pl.ds((bands + 1) * prows, pad), :] = jnp.zeros((pad, LANES), jnp.float32)
    strips[pl.ds(pl.multiple_of((me + 1) * prows, prows), prows), :] = strip_ref[...]
    cpad = (cbuf.shape[2] - bands * tile) // 2
    blank = jnp.zeros((span // LANES, 3, cpad, LANES), jnp.float32)
    cbuf[:, :, pl.ds(0, cpad), :] = blank
    cbuf[:, :, pl.ds(cpad + bands * tile, cpad), :] = blank

    def recv_strip(j, _):
        strip_copy(lax.rem(me + j, bands), me, j).wait_recv()
        return 0

    lax.fori_loop(1, bands, recv_strip, 0)

    g = strips[...]
    lane = iota((1, LANES), 1)
    turn = lane_roll(g, -16)
    height = g + jnp.where(lane < 16, -half, courant * half) * (row_roll(turn, -1) - row_roll(turn, 1))
    turn = lane_roll(height, 64)
    columns = jnp.where(lane < 64, height, g - half * (row_roll(turn, -1) - row_roll(turn, 1)))

    acc[...] = jnp.zeros_like(acc)

    def add_end(k, _):
        @pl.when(k > 0)
        def _():
            end_copy(0, k, 0).wait_recv()

        acc[...] += endbuf[k]
        return 0

    ends_lane = span + LANES

    @pl.when(first)
    def _():
        endbuf[0] = ends_ref[0]

    @pl.when(last)
    def _():
        endbuf[0] = ends_ref[1]

    @pl.when(jnp.logical_or(first, last))
    def _():
        lax.fori_loop(0, top_senders, add_end, 0)

    j = iota((ends_lane, nwidth), 1) + 2
    q, t = j // 3, j % 3
    k = iota((ends_lane, nwidth), 0) - 3
    fine = jnp.where(k == q, (3 - t).astype(jnp.float32) / 3.0, 0.0) + jnp.where(
        k == q + 1, t.astype(jnp.float32) / 3.0, 0.0
    )
    summed = acc[...].reshape(3 * members, ends_lane)
    ghost_rows = jnp.dot(summed, fine, precision=highest, preferred_element_type=jnp.float32)
    ghost[...] = ghost_rows.reshape(3, members, nwidth)

    own.wait()

    @pl.when(jnp.logical_not(first))
    def _():
        nest_down(me).wait_recv()

    @pl.when(jnp.logical_not(last))
    def _():
        nest_up(me).wait_recv()

    erows = nrows + 2 * HALO
    row = iota((erows, nwidth), 0)
    col = iota((erows, nwidth), 1)
    is_ghost = jnp.logical_or(
        jnp.logical_and(row == HALO - 1, first), jnp.logical_and(row == HALO + nrows, last)
    )
    at_west, at_east = col == 0, col == nwidth - 1
    total_rows = strips.shape[0]
    n = iota((erows, total_rows), 0) + (me * nrows - HALO + 2 + 9)
    wq, wt = n // 3 - 3, n % 3
    lower = (3 - wt).astype(jnp.float32) / 3.0
    upper = wt.astype(jnp.float32) / 3.0
    prow = iota((erows, total_rows), 1) - prows
    lanes = iota((erows, LANES), 1)
    pick_rows = iota((tile, erows), 1) - HALO
    pick = jnp.where(pick_rows // 3 == iota((tile, erows), 0), 1.0, 0.0)
    pick = jnp.where(pick_rows >= 0, pick, 0.0)

    def one_member(mem, _):
        row0 = off_ref[mem, 0]
        rel = prow - row0 + 1
        weights = jnp.where(rel == wq, lower, 0.0) + jnp.where(rel == wq + 1, upper, 0.0)
        side = jnp.dot(weights, columns, precision=highest, preferred_element_type=jnp.float32)

        def side_of(f, s):
            return jnp.sum(jnp.where(lanes == 32 * f + s + 2 * mem, side, 0.0), axis=1, keepdims=True)

        sides = [[side_of(f, s) for s in range(2)] for f in range(2)]
        ends = [ghost[f, pl.ds(mem, 1), :] for f in range(3)]

        def ddx(x, f):
            left = jnp.where(at_west, sides[f][0], lane_roll(x, 1))
            right = jnp.where(at_east, sides[f][1], lane_roll(x, -1))
            return right - left

        def ddy(x):
            return row_roll(x, -1) - row_roll(x, 1)

        def bound(x, f):
            return jnp.where(is_ghost, ends[f], x)

        h, z, m = ext[mem, 0], bound(ext[mem, 1], 1), bound(ext[mem, 2], 2)
        for _ in range(NSTEPS):
            h = bound(h - half * (ddx(z, 1) + ddy(m)), 0)
            z, m = (
                bound(keep * z - half * ddx(h, 0) + rotation * m, 1),
                bound(keep * m - half * ddy(h) - rotation * z, 2),
            )
        for f, x in enumerate((h, z, m)):
            nest_out[mem, f] = x[HALO : HALO + nrows]
            x = jnp.where(jnp.logical_and(row >= HALO, row < HALO + nrows), x, 0.0)
            coarse[mem, f, :, :] = jnp.dot(pick, x, precision=highest, preferred_element_type=jnp.float32)
        return 0

    lax.fori_loop(0, members, one_member, 0)

    thin = jnp.where(
        iota((nwidth, span), 0) // 3 == iota((nwidth, span), 1), 1.0 / 9.0, 0.0
    )
    block = coarse[...].reshape(members * 3 * tile, nwidth)
    means = jnp.dot(block, thin, precision=highest, preferred_element_type=jnp.float32)
    for k in range(0, span, LANES):
        dealt[:, k // LANES] = means[:, k : k + LANES].reshape(members, 3, tile, LANES)

    turn_of = lax.rem(group, per)

    def mid_copy(mem, slot, to):
        return remote(
            dealt.at[mem],
            cbuf.at[:, :, pl.ds(pl.multiple_of(cpad + slot * tile, tile), tile), :],
            mid_send.at[mem],
            mid_recv.at[slot],
            to,
        )

    def to_mid(mem, _):
        to = per * mem + turn_of

        @pl.when(to != me)
        def _():
            mid_copy(mem, me, to).start()

        @pl.when(to == me)
        def _():
            cbuf[:, :, pl.ds(pl.multiple_of(cpad + me * tile, tile), tile), :] = dealt[mem]

        return 0

    lax.fori_loop(0, members, to_mid, 0)
    is_mid = lax.rem(me, per) == turn_of
    mine = me // per

    def out_copy(to):
        return remote(sbuf.at[to], patch.at[mine], out_send.at[to], out_recv.at[mine], to)

    @pl.when(is_mid)
    def _():
        def recv(j, _):
            mid_copy(0, lax.rem(me + j, bands), me).wait_recv()
            return 0

        lax.fori_loop(1, bands, recv, 0)
        start_row = off_ref[mine, 0]

        def deal(j, _):
            to = lax.rem(me + j, bands)
            begin = jnp.clip(to * prows - start_row, -cpad, bands * tile) + cpad
            for k in range(0, span, LANES):
                sbuf[to, :, :, pl.ds(k, LANES)] = cbuf[k // LANES, :, pl.ds(begin, prows), :]

            @pl.when(to != me)
            def _():
                out_copy(to).start()

            return 0

        lax.fori_loop(1, bands + 1, deal, 0)
        patch[mine] = sbuf[me]

    def recv_patch(mem, _):
        @pl.when(per * mem + turn_of != me)
        def _():
            remote(sbuf.at[0], patch.at[mem], out_send.at[0], out_recv.at[mem], me).wait_recv()

        return 0

    lax.fori_loop(0, members, recv_patch, 0)

    @pl.when(jnp.logical_not(first))
    def _():
        edge_down(me).wait_recv()
        edge_up(me).wait_send()
        nest_up(me).wait_send()

    @pl.when(jnp.logical_not(last))
    def _():
        edge_up(me).wait_recv()
        edge_down(me).wait_send()
        nest_down(me).wait_send()

    @pl.when(sends_top)
    def _():
        end_copy(0, me, 0).wait_send()

    @pl.when(sends_bottom)
    def _():
        end_copy(1, bands - 1 - me, bands - 1).wait_send()

    def sent_strip(j, _):
        strip_copy(me, lax.rem(me + j, bands), j).wait_send()
        return 0

    lax.fori_loop(1, bands, sent_strip, 0)

    def sent_mid(mem, _):
        @pl.when(per * mem + turn_of != me)
        def _():
            mid_copy(mem, me, me).wait_send()

        return 0

    lax.fori_loop(0, members, sent_mid, 0)

    @pl.when(is_mid)
    def _():
        def sent_out(j, _):
            out_copy(lax.rem(me + j, bands)).wait_send()
            return 0

        lax.fori_loop(1, bands, sent_out, 0)


def parent_kernel(span, bands, off_ref, band_ref, par_ref, halo_ref, patch_ref, out_ref):
    mem = pl.program_id(0)
    rows, width = par_ref.shape[2], par_ref.shape[3]
    row0, col0 = off_ref[mem, 0], off_ref[mem, 1]
    band = band_ref[0]
    first, last = band == 0, band == bands - 1
    h, z, m = par_ref[0, 0], par_ref[0, 1], par_ref[0, 2]
    row = iota(h.shape, 0)

    def ddy(x, above, below):
        up = jnp.where(row == 0, above, row_roll(x, 1))
        down = jnp.where(row == rows - 1, below, row_roll(x, -1))
        return down - up

    m_above = jnp.where(first, 0.0, halo_ref[0, 0, 0:1, :])
    m_below = jnp.where(last, 0.0, halo_ref[1, 0, 0:1, :])
    h_above = jnp.where(first, 0.0, halo_ref[0, 0, 1:2, :] - half * m[0:1])
    h_below = jnp.where(last, 0.0, halo_ref[1, 0, 1:2, :] + half * m[rows - 1 : rows])
    h1 = h - courant * dx(z) - half * ddy(m, m_above, m_below)
    out_ref[0, 0] = h1
    out_ref[0, 1] = keep * z - courant * dx(h1) + rotation * m
    out_ref[0, 2] = keep * m - half * ddy(h1, h_above, h_below) - rotation * z

    block0 = col0 // LANES
    shift = col0 - block0 * LANES
    place = pl.ds(pl.multiple_of(block0 * LANES, LANES), span + LANES)
    wide = jnp.concatenate([patch_ref[0], jnp.zeros((3, rows, LANES), jnp.float32)], axis=-1)
    wide = pltpu.roll(wide.reshape(3 * rows, span + LANES), shift, 1).reshape(3, rows, span + LANES)
    lane = iota(wide.shape, 2)
    at = iota(wide.shape, 1) + (band * rows - row0)
    inside = (lane >= shift) & (lane < shift + span) & (at >= 0) & (at < span)
    out_ref[0, :, :, place] = jnp.where(inside, wide, out_ref[0, :, :, place])


def per_device(bands, parent_state, nest_state, offsets):
    members, _, prows, width = parent_state.shape
    nrows, nwidth = nest_state.shape[2:]
    span = nwidth // 3
    tile = nrows // 3
    f32 = jnp.float32
    band = lax.axis_index("band").reshape(1).astype(jnp.int32)
    shape = jax.ShapeDtypeStruct
    limit = 48 * 1024 * 1024
    parent_spec = pl.BlockSpec((1, 3, prows, width), lambda i, *_: (i, 0, 0, 0))
    edge_spec = pl.BlockSpec((2, 1, 2, width), lambda i, *_: (0, i, 0, 0))

    edges, strip, ends = pl.pallas_call(
        functools.partial(gather_kernel, span, bands),
        out_shape=(
            shape((2, members, 2, width), f32),
            shape((prows, LANES), f32),
            shape((2, 3, members, span + LANES), f32),
        ),
        grid_spec=pltpu.PrefetchScalarGridSpec(
            num_scalar_prefetch=2,
            grid=(members,),
            in_specs=[parent_spec],
            out_specs=(
                edge_spec,
                pl.BlockSpec((prows, LANES), lambda i, *_: (0, 0)),
                pl.BlockSpec((2, 3, members, span + LANES), lambda i, *_: (0, 0, 0, 0)),
            ),
        ),
        compiler_params=pltpu.CompilerParams(vmem_limit_bytes=limit),
        name="gather",
    )(offsets, band, parent_state)

    vmem = pl.BlockSpec(memory_space=pltpu.VMEM)
    hbm = pl.BlockSpec(memory_space=pl.ANY)
    dma = pltpu.SemaphoreType.DMA
    senders = bands // 2 + 1
    nest_out, patch, halo = pl.pallas_call(
        functools.partial(nest_kernel, bands, span),
        out_shape=(
            shape(nest_state.shape, f32),
            shape((members, 3, prows, span), f32),
            shape((2, members, 2, width), f32),
        ),
        in_specs=[pl.BlockSpec(memory_space=pltpu.SMEM), hbm, hbm, vmem, vmem],
        out_specs=(vmem, vmem, hbm),
        scratch_shapes=[
            pltpu.VMEM((members, 3, nrows + 2 * HALO, nwidth), f32),
            pltpu.VMEM(((bands + 2) * prows, LANES), f32),
            pltpu.VMEM((senders, 3, members, span + LANES), f32),
            pltpu.VMEM((3, members, nwidth), f32),
            pltpu.VMEM((3, members, span + LANES), f32),
            pltpu.VMEM((members, 3, tile, nwidth), f32),
            pltpu.VMEM((members, span // LANES, 3, tile, LANES), f32),
            pltpu.VMEM((span // LANES, 3, bands * tile + 2 * prows, LANES), f32),
            pltpu.VMEM((bands, 3, prows, span), f32),
            dma((2,)),
            dma((2,)),
            dma((2,)),
            dma((2,)),
            dma((bands,)),
            dma((bands,)),
            dma((2,)),
            dma((senders,)),
            dma((members,)),
            dma((bands,)),
            dma((bands,)),
            dma((members,)),
            dma,
        ],
        compiler_params=pltpu.CompilerParams(collective_id=0, has_side_effects=True, vmem_limit_bytes=limit),
        name="nest",
    )(offsets, nest_state, edges, strip, ends)

    parent_out = pl.pallas_call(
        functools.partial(parent_kernel, span, bands),
        out_shape=shape(parent_state.shape, f32),
        grid_spec=pltpu.PrefetchScalarGridSpec(
            num_scalar_prefetch=2,
            grid=(members,),
            in_specs=[
                parent_spec,
                edge_spec,
                pl.BlockSpec((1, 3, prows, span), lambda i, *_: (i, 0, 0, 0)),
            ],
            out_specs=parent_spec,
        ),
        compiler_params=pltpu.CompilerParams(vmem_limit_bytes=limit),
        name="parent",
    )(offsets, band, parent_state, halo, patch)
    return (parent_out, nest_out)


def solution(mesh):
    in_specs = (P("member", None, "band", None), P("member", None, "band", None), P("member", None))
    out_specs = (P("member", None, "band", None), P("member", None, "band", None))
    return jax.shard_map(
        functools.partial(per_device, mesh.shape["band"]),
        mesh=mesh,
        in_specs=in_specs,
        out_specs=out_specs,
        check_vma=False,
    )
```

time: 480 us -> 68.9 us (0.14); the launches traced: 473 us -> 68.4 us
  local copies, waits for them, and re-layouts: 179 us -> 1.75 us
  other arithmetic: 96.7 us -> 0 us
  waiting for transfers between devices: 81.5 us -> 0 us
  Pallas kernels: 0 us -> 66 us
  starting transfers between devices: 49.2 us -> 0 us
  blocking collectives: 47.1 us -> 0 us
  between operations: 14.9 us -> 0.67 us
  matrix products: 4.82 us -> 0 us
    pallas_call x0 -> x3, Pallas kernels: none -> 66 us  [the longest x1 48.2 us: per_device(): pl.pallas_call(functools.partial(nest_kernel, bands, span), out_shape=(sh...]
    all_gather x1 -> x0, waiting for transfers between devices: 60.8 us -> none  [per_device(): whole = lax.all_gather(coarse, 'band', axis=2, tiled=True)]
    another operation x10 -> x0, local copies, waits for them, and re-layouts: 55.2 us -> none  [the longest x1 48.6 us: per_device(): stepped = jnp.stack([height_new, zonal_new, merid_new], axis=1)]
    ppermute x16 -> x0, starting transfers between devices: 49.1 us -> none  [the longest x8 38.5 us: with_halo(): lax.ppermute(tail, axis, [(i, (i + 1) % count) for i in range(ends)])]
    scatter x17 -> x0, other arithmetic: 47.9 us -> none
    all_gather x1 -> x0, blocking collectives: 47.1 us -> none  [per_device(): column_all = lax.all_gather(strip, 'band', axis=3, tiled=True)]
    psum x1 -> x0, local copies, waits for them, and re-layouts: 36.1 us -> none  [per_device(): ends_full = lax.psum(partial_rows, 'band')]
    scatter x24 -> x0, local copies, waits for them, and re-layouts: 29.9 us -> none
  transfers between devices with their start and end apart: 18 -> 0, of which waited for: 7 -> 0; matrix products, arithmetic and copies ran while one was open for 33% -> 0% of each run, Pallas kernels for 0% -> 0%
where the time goes in v1:
time: 68.9 us; the launch traced here: 68.4 us
  Pallas kernels  66 us (96%)
  local copies, waits for them, and re-layouts  1.75 us (3%)
    pallas_call x1, Pallas kernels, per_device(): pl.pallas_call(functools.partial(nest_kernel, bands, span), out_shape=(sh...  48.2 us
    pallas_call x1, Pallas kernels, per_device(): pl.pallas_call(functools.partial(parent_kernel, span, bands), out_shape=s...  9.86 us
    pallas_call x1, Pallas kernels, per_device(): pl.pallas_call(functools.partial(gather_kernel, span, bands), out_shape=(...  7.92 us
    unnamed x4, local copies, waits for them, and re-layouts  1.75 us

profile of v1, /device:TPU:0, one launch (start us, length us, event | category | flops | bytes accessed | tf_op | source)
XLA Modules:
  0.0 68.4 jit_solution(1003974343887179433)
XLA Ops:
  0.6 0.0 copy-start
  0.6 0.8 %copy.7.off_ref = s32[8,2]{1,0:T(8,128)S(1)} copy(s32[8,2]{0,1:T(2,128)} %param.5) | data formatting | bytes 128 | tf_op args[2]
  1.5 7.9 %gather.1 = (f32[2,8,2,4096]{3,2,1,0:T(2,128)S(1)}, f32[16,128]{1,0:T(8,128)S(1)}, f32[2,3,8,256]{3,2,1,0:T(8,128)S(1)}) custom-call(s32[8,2]{1,0:T(8,128)S(1)} %copy.7.off_ref, s32[1]{0:T(128)} %bitcast.band_ref, f32[8,3,16,4096]{3,2,1,0:T(8,128)} %par_ref.3), custom_call_target="tpu_custom_call" | custom-call | tf_op jit(solution)/shard_map/gather/pallas_call | solution.py:512
  9.4 0.0 copy-done
  9.4 48.2 %nest.1 = (f32[8,3,24,384]{3,2,1,0:T(8,128)S(1)}, f32[8,3,16,128]{3,2,1,0:T(8,128)S(1)}, f32[2,8,2,4096]{3,2,1,0:T(2,128)S(1)}) custom-call(s32[8,2]{1,0:T(8,128)S(1)} %copy.7.off_ref, f32[8,3,24,384]{3,2,1,0:T(8,128)S(1)} %copy-done, f32[2,8,2,4096]{3,2,1,0:T(2,128)S(1)} %get-tuple-element.8.edge_ref, f32[16,128]{1,0:T(8,128)S(1)} %get-tuple-element.9.strip_ref, ...), custom_call_target="tpu_custom_call" | custom-call | tf_op jit(solution)/shard_map/nest/pallas_call | solution.py:537
  57.7 9.9 %parent.1 = f32[8,3,16,4096]{3,2,1,0:T(8,128)} custom-call(s32[8,2]{1,0:T(8,128)S(1)} %copy.7.off_ref, s32[1]{0:T(128)} %bitcast.band_ref, f32[8,3,16,4096]{3,2,1,0:T(8,128)} %par_ref.3, f32[2,8,2,4096]{3,2,1,0:T(2,128)S(1)} %get-tuple-element.11.halo_ref, f32[8,3,16,128]{3,2,1,0:T(8,128)S(1)} %get-tuple-element.12.patch_ref), custom_call_target="tpu_custom_call" | custom-call | tf_op jit(solution)/shard_map/parent/pallas_call | solution.py:574
  67.5 0.9 %copy.9 = f32[8,3,24,384]{3,2,1,0:T(8,128)} copy(f32[8,3,24,384]{3,2,1,0:T(8,128)S(1)} %get-tuple-element.17) | data formatting | bytes 1769472
Async XLA Ops:
  0.6 8.8 %copy-start = (f32[8,3,24,384]{3,2,1,0:T(8,128)S(1)}, f32[8,3,24,384]{3,2,1,0:T(8,128)}, u32[]{:S(2)}) copy-start(f32[8,3,24,384]{3,2,1,0:T(8,128)} %nest_ref.1) | copy-start | bytes 2654212

commit v2 on v1

--- a/solution.py
+++ b/solution.py
@@ -36,6 +36,17 @@
 
 def iota(shape, dim):
     return lax.broadcasted_iota(jnp.int32, shape, dim)
+
+
+def split(x):
+    high = x.astype(jnp.bfloat16)
+    rest = x - high.astype(jnp.float32)
+    mid = rest.astype(jnp.bfloat16)
+    return high, mid, (rest - mid.astype(jnp.float32)).astype(jnp.bfloat16)
+
+
+def exact_dot(x, weights):
+    return sum(jnp.dot(part, weights, preferred_element_type=jnp.float32) for part in split(x))
 
 
 def gather_kernel(span, bands, off_ref, band_ref, par_ref, edge_ref, strip_ref, ends_ref):
@@ -120,9 +131,12 @@
     ext,
     strips,
     endbuf,
+    cols,
+    side,
     ghost,
     acc,
-    coarse,
+    fine,
+    thinned,
     dealt,
     cbuf,
     sbuf,
@@ -164,20 +178,26 @@
     own.start()
     pl.semaphore_wait(barrier, bands - 1)
 
-    def nest_down(to):
+    reach = 2 * NSTEPS
+
+    def nest_down(mem, to):
         return remote(
-            nest_ref.at[:, :, pl.ds(nrows - HALO, HALO), :], ext.at[:, :, pl.ds(0, HALO), :], nest_send.at[0], nest_recv.at[0], to
-        )
-
-    def nest_up(to):
-        return remote(
-            nest_ref.at[:, :, pl.ds(0, HALO), :],
-            ext.at[:, :, pl.ds(HALO + nrows, HALO), :],
-            nest_send.at[1],
-            nest_recv.at[1],
+            nest_ref.at[mem, :, pl.ds(nrows - reach, reach), :],
+            ext.at[mem, :, pl.ds(HALO - reach, reach), :],
+            nest_send.at[0, mem],
+            nest_recv.at[0, mem],
             to,
         )
 
+    def nest_up(mem, to):
+        return remote(
+            nest_ref.at[mem, :, pl.ds(0, reach), :],
+            ext.at[mem, :, pl.ds(HALO + nrows, reach), :],
+            nest_send.at[1, mem],
+            nest_recv.at[1, mem],
+            to,
+        )
+
     def edge_down(to):
         return remote(edge_ref.at[1], halo.at[0], edge_send.at[0], edge_recv.at[0], to)
 
@@ -192,14 +212,6 @@
 
     first, last = me == 0, me == bands - 1
 
-    @pl.when(jnp.logical_not(first))
-    def _():
-        nest_up(me - 1).start()
-
-    @pl.when(jnp.logical_not(last))
-    def _():
-        nest_down(me + 1).start()
-
     def send_strip(j, _):
         strip_copy(me, lax.rem(me + j, bands), j).start()
         return 0
@@ -216,6 +228,19 @@
     @pl.when(sends_bottom)
     def _():
         end_copy(1, bands - 1 - me, bands - 1).start()
+
+    def send_nest(mem, _):
+        @pl.when(jnp.logical_not(first))
+        def _():
+            nest_up(mem, me - 1).start()
+
+        @pl.when(jnp.logical_not(last))
+        def _():
+            nest_down(mem, me + 1).start()
+
+        return 0
+
+    lax.fori_loop(0, members, send_nest, 0)
 
     @pl.when(jnp.logical_not(first))
     def _():
@@ -234,126 +259,74 @@
     cbuf[:, :, pl.ds(0, cpad), :] = blank
     cbuf[:, :, pl.ds(cpad + bands * tile, cpad), :] = blank
 
-    def recv_strip(j, _):
-        strip_copy(lax.rem(me + j, bands), me, j).wait_recv()
-        return 0
-
-    lax.fori_loop(1, bands, recv_strip, 0)
-
-    g = strips[...]
-    lane = iota((1, LANES), 1)
-    turn = lane_roll(g, -16)
-    height = g + jnp.where(lane < 16, -half, courant * half) * (row_roll(turn, -1) - row_roll(turn, 1))
-    turn = lane_roll(height, 64)
-    columns = jnp.where(lane < 64, height, g - half * (row_roll(turn, -1) - row_roll(turn, 1)))
-
-    acc[...] = jnp.zeros_like(acc)
-
-    def add_end(k, _):
-        @pl.when(k > 0)
-        def _():
-            end_copy(0, k, 0).wait_recv()
-
-        acc[...] += endbuf[k]
-        return 0
-
     ends_lane = span + LANES
 
-    @pl.when(first)
-    def _():
-        endbuf[0] = ends_ref[0]
-
-    @pl.when(last)
-    def _():
-        endbuf[0] = ends_ref[1]
-
     @pl.when(jnp.logical_or(first, last))
     def _():
-        lax.fori_loop(0, top_senders, add_end, 0)
-
-    j = iota((ends_lane, nwidth), 1) + 2
-    q, t = j // 3, j % 3
-    k = iota((ends_lane, nwidth), 0) - 3
-    fine = jnp.where(k == q, (3 - t).astype(jnp.float32) / 3.0, 0.0) + jnp.where(
+        j = iota((1, nwidth), 1) + 2
+        q, t = j // 3, j % 3
+        k = iota((ends_lane, nwidth), 0) - 3
+        fine[...] = (jnp.where(k == q, 3 - t, 0) + jnp.where(k == q + 1, t, 0)).astype(jnp.float32).astype(jnp.bfloat16)
+
+    erows = nrows + 2 * HALO
+    e = iota((erows, prows), 0)
+    q, t = e // 3, e % 3
+    k = iota((erows, prows), 1)
+    weights = jnp.where(k == q, (3 - t).astype(jnp.float32) / 3.0, 0.0) + jnp.where(
         k == q + 1, t.astype(jnp.float32) / 3.0, 0.0
     )
-    summed = acc[...].reshape(3 * members, ends_lane)
-    ghost_rows = jnp.dot(summed, fine, precision=highest, preferred_element_type=jnp.float32)
-    ghost[...] = ghost_rows.reshape(3, members, nwidth)
-
-    own.wait()
-
-    @pl.when(jnp.logical_not(first))
-    def _():
-        nest_down(me).wait_recv()
-
-    @pl.when(jnp.logical_not(last))
-    def _():
-        nest_up(me).wait_recv()
-
-    erows = nrows + 2 * HALO
+    thin = jnp.where(iota((nwidth, span), 0) // 3 == iota((nwidth, span), 1), 1.0, 0.0).astype(jnp.bfloat16)
     row = iota((erows, nwidth), 0)
     col = iota((erows, nwidth), 1)
     is_ghost = jnp.logical_or(
         jnp.logical_and(row == HALO - 1, first), jnp.logical_and(row == HALO + nrows, last)
     )
     at_west, at_east = col == 0, col == nwidth - 1
-    total_rows = strips.shape[0]
-    n = iota((erows, total_rows), 0) + (me * nrows - HALO + 2 + 9)
-    wq, wt = n // 3 - 3, n % 3
-    lower = (3 - wt).astype(jnp.float32) / 3.0
-    upper = wt.astype(jnp.float32) / 3.0
-    prow = iota((erows, total_rows), 1) - prows
     lanes = iota((erows, LANES), 1)
-    pick_rows = iota((tile, erows), 1) - HALO
-    pick = jnp.where(pick_rows // 3 == iota((tile, erows), 0), 1.0, 0.0)
-    pick = jnp.where(pick_rows >= 0, pick, 0.0)
-
-    def one_member(mem, _):
-        row0 = off_ref[mem, 0]
-        rel = prow - row0 + 1
-        weights = jnp.where(rel == wq, lower, 0.0) + jnp.where(rel == wq + 1, upper, 0.0)
-        side = jnp.dot(weights, columns, precision=highest, preferred_element_type=jnp.float32)
-
-        def side_of(f, s):
-            return jnp.sum(jnp.where(lanes == 32 * f + s + 2 * mem, side, 0.0), axis=1, keepdims=True)
-
-        sides = [[side_of(f, s) for s in range(2)] for f in range(2)]
-        ends = [ghost[f, pl.ds(mem, 1), :] for f in range(3)]
-
-        def ddx(x, f):
-            left = jnp.where(at_west, sides[f][0], lane_roll(x, 1))
-            right = jnp.where(at_east, sides[f][1], lane_roll(x, -1))
-            return right - left
-
-        def ddy(x):
-            return row_roll(x, -1) - row_roll(x, 1)
-
-        def bound(x, f):
-            return jnp.where(is_ghost, ends[f], x)
-
-        h, z, m = ext[mem, 0], bound(ext[mem, 1], 1), bound(ext[mem, 2], 2)
-        for _ in range(NSTEPS):
-            h = bound(h - half * (ddx(z, 1) + ddy(m)), 0)
-            z, m = (
-                bound(keep * z - half * ddx(h, 0) + rotation * m, 1),
-                bound(keep * m - half * ddy(h) - rotation * z, 2),
-            )
-        for f, x in enumerate((h, z, m)):
-            nest_out[mem, f] = x[HALO : HALO + nrows]
-            x = jnp.where(jnp.logical_and(row >= HALO, row < HALO + nrows), x, 0.0)
-            coarse[mem, f, :, :] = jnp.dot(pick, x, precision=highest, preferred_element_type=jnp.float32)
-        return 0
-
-    lax.fori_loop(0, members, one_member, 0)
-
-    thin = jnp.where(
-        iota((nwidth, span), 0) // 3 == iota((nwidth, span), 1), 1.0 / 9.0, 0.0
-    )
-    block = coarse[...].reshape(members * 3 * tile, nwidth)
-    means = jnp.dot(block, thin, precision=highest, preferred_element_type=jnp.float32)
-    for k in range(0, span, LANES):
-        dealt[:, k // LANES] = means[:, k : k + LANES].reshape(members, 3, tile, LANES)
+
+    def recv_strip(j, _):
+        strip_copy(lax.rem(me + j, bands), me, j).wait_recv()
+        return 0
+
+    lax.fori_loop(1, bands, recv_strip, 0)
+
+    g = strips[...]
+    lane = iota((1, LANES), 1)
+    turn = lane_roll(g, -16)
+    height = g + jnp.where(lane < 16, -half, courant * half) * (row_roll(turn, -1) - row_roll(turn, 1))
+    turn = lane_roll(height, 64)
+    cols[...] = jnp.where(lane < 64, height, g - half * (row_roll(turn, -1) - row_roll(turn, 1)))
+    picked = jnp.zeros((prows, LANES), jnp.float32)
+    for mem in range(members):
+        begin = off_ref[mem, 0] + (me * tile - 3 + prows)
+        picked = jnp.where(lane % 32 // 2 == mem, cols[pl.ds(begin, prows), :], picked)
+    side[...] = jnp.dot(weights, picked, precision=highest, preferred_element_type=jnp.float32)
+
+
+    def add_end(k, _):
+        @pl.when(k > 0)
+        def _():
+            end_copy(0, k, 0).wait_recv()
+
+        acc[...] += endbuf[k]
+        return 0
+
+    @pl.when(first)
+    def _():
+        endbuf[0] = ends_ref[0]
+
+    @pl.when(last)
+    def _():
+        endbuf[0] = ends_ref[1]
+
+    @pl.when(jnp.logical_or(first, last))
+    def _():
+        acc[...] = jnp.zeros_like(acc)
+        lax.fori_loop(0, top_senders, add_end, 0)
+        rows_in = acc[...].reshape(3 * members, ends_lane)
+        ghost[...] = (exact_dot(rows_in, fine[...]) * (1.0 / 3.0)).reshape(3, members, nwidth)
+
+    own.wait()
 
     turn_of = lax.rem(group, per)
 
@@ -366,7 +339,48 @@
             to,
         )
 
-    def to_mid(mem, _):
+    def one_member(mem, _):
+        @pl.when(jnp.logical_not(first))
+        def _():
+            nest_down(mem, me).wait_recv()
+
+        @pl.when(jnp.logical_not(last))
+        def _():
+            nest_up(mem, me).wait_recv()
+
+        def side_of(f, s):
+            return jnp.sum(jnp.where(lanes == 32 * f + s + 2 * mem, side[...], 0.0), axis=1, keepdims=True)
+
+        sides = [[side_of(f, s) for s in range(2)] for f in range(2)]
+        ends = [ghost[f, pl.ds(mem, 1), :] for f in range(3)]
+
+        def ddx(x, f):
+            left = jnp.where(at_west, sides[f][0], lane_roll(x, 1))
+            right = jnp.where(at_east, sides[f][1], lane_roll(x, -1))
+            return right - left
+
+        def ddy(x):
+            return row_roll(x, -1) - row_roll(x, 1)
+
+        def bound(x, f):
+            return jnp.where(is_ghost, ends[f], x)
+
+        h, z, m = ext[mem, 0], bound(ext[mem, 1], 1), bound(ext[mem, 2], 2)
+        for _ in range(NSTEPS):
+            h = bound(h - half * (ddx(z, 1) + ddy(m)), 0)
+            z, m = (
+                bound(keep * z - half * ddx(h, 0) + rotation * m, 1),
+                bound(keep * m - half * ddy(h) - rotation * z, 2),
+            )
+        inner = [x[HALO : HALO + nrows] for x in (h, z, m)]
+        for f, x in enumerate(inner):
+            nest_out[mem, f] = x
+        sums = exact_dot(jnp.concatenate(inner, axis=0), thin)
+        for k in range(span // LANES):
+            thinned[k] = sums[:, k * LANES : (k + 1) * LANES]
+            for f in range(3):
+                parts = [thinned[k, pl.ds(f * nrows + i, tile, stride=3), :] for i in range(3)]
+                dealt[mem, k, f] = (parts[0] + parts[1] + parts[2]) * (1.0 / 9.0)
         to = per * mem + turn_of
 
         @pl.when(to != me)
@@ -379,7 +393,7 @@
 
         return 0
 
-    lax.fori_loop(0, members, to_mid, 0)
+    lax.fori_loop(0, members, one_member, 0)
     is_mid = lax.rem(me, per) == turn_of
     mine = me // per
 
@@ -423,13 +437,11 @@
     def _():
         edge_down(me).wait_recv()
         edge_up(me).wait_send()
-        nest_up(me).wait_send()
 
     @pl.when(jnp.logical_not(last))
     def _():
         edge_up(me).wait_recv()
         edge_down(me).wait_send()
-        nest_down(me).wait_send()
 
     @pl.when(sends_top)
     def _():
@@ -446,6 +458,14 @@
     lax.fori_loop(1, bands, sent_strip, 0)
 
     def sent_mid(mem, _):
+        @pl.when(jnp.logical_not(first))
+        def _():
+            nest_up(mem, me).wait_send()
+
+        @pl.when(jnp.logical_not(last))
+        def _():
+            nest_down(mem, me).wait_send()
+
         @pl.when(per * mem + turn_of != me)
         def _():
             mid_copy(mem, me, me).wait_send()
@@ -547,14 +567,17 @@
             pltpu.VMEM((members, 3, nrows + 2 * HALO, nwidth), f32),
             pltpu.VMEM(((bands + 2) * prows, LANES), f32),
             pltpu.VMEM((senders, 3, members, span + LANES), f32),
+            pltpu.VMEM(((bands + 2) * prows, LANES), f32),
+            pltpu.VMEM((nrows + 2 * HALO, LANES), f32),
             pltpu.VMEM((3, members, nwidth), f32),
             pltpu.VMEM((3, members, span + LANES), f32),
-            pltpu.VMEM((members, 3, tile, nwidth), f32),
+            pltpu.VMEM((span + LANES, nwidth), jnp.bfloat16),
+            pltpu.VMEM((span // LANES, 3 * nrows, LANES), f32),
             pltpu.VMEM((members, span // LANES, 3, tile, LANES), f32),
             pltpu.VMEM((span // LANES, 3, bands * tile + 2 * prows, LANES), f32),
             pltpu.VMEM((bands, 3, prows, span), f32),
-            dma((2,)),
-            dma((2,)),
+            dma((2, members)),
+            dma((2, members)),
             dma((2,)),
             dma((2,)),
             dma((bands,)),

time: 68.9 us -> 59.4 us (0.86)
  Pallas kernels: 66 us -> 56.5 us
    pallas_call x1, Pallas kernels: 48.2 us -> 38.8 us  [per_device(): pl.pallas_call(functools.partial(nest_kernel, bands, span), out_shape=(sh...]
where the time goes in v2:
time: 59.4 us; the launch traced here: 59 us
  Pallas kernels  56.5 us (95%)
  local copies, waits for them, and re-layouts  1.75 us (3%)
  between operations  0.67 us (1%)
    pallas_call x1, Pallas kernels, per_device(): pl.pallas_call(functools.partial(nest_kernel, bands, span), out_shape=(sh...  38.8 us
    pallas_call x1, Pallas kernels, per_device(): pl.pallas_call(functools.partial(parent_kernel, span, bands), out_shape=s...  9.86 us
    pallas_call x1, Pallas kernels, per_device(): pl.pallas_call(functools.partial(gather_kernel, span, bands), out_shape=(...  7.92 us
    unnamed x4, local copies, waits for them, and re-layouts  1.75 us

profile of v2, /device:TPU:0, one launch (start us, length us, event | category | flops | bytes accessed | tf_op | source)
XLA Modules:
  0.0 59.0 jit_solution(6625143957062083777)
XLA Ops:
  0.6 0.0 copy-start
  0.6 0.8 %copy.7.off_ref = s32[8,2]{1,0:T(8,128)S(1)} copy(s32[8,2]{0,1:T(2,128)} %param.5) | data formatting | bytes 128 | tf_op args[2]
  1.5 7.9 %gather.1 = (f32[2,8,2,4096]{3,2,1,0:T(2,128)S(1)}, f32[16,128]{1,0:T(8,128)S(1)}, f32[2,3,8,256]{3,2,1,0:T(8,128)S(1)}) custom-call(s32[8,2]{1,0:T(8,128)S(1)} %copy.7.off_ref, s32[1]{0:T(128)} %bitcast.band_ref, f32[8,3,16,4096]{3,2,1,0:T(8,128)} %par_ref.3), custom_call_target="tpu_custom_call" | custom-call | tf_op jit(solution)/shard_map/gather/pallas_call | solution.py:532
  9.4 0.0 copy-done
  9.4 38.8 %nest.1 = (f32[8,3,24,384]{3,2,1,0:T(8,128)S(1)}, f32[8,3,16,128]{3,2,1,0:T(8,128)S(1)}, f32[2,8,2,4096]{3,2,1,0:T(2,128)S(1)}) custom-call(s32[8,2]{1,0:T(8,128)S(1)} %copy.7.off_ref, f32[8,3,24,384]{3,2,1,0:T(8,128)S(1)} %copy-done, f32[2,8,2,4096]{3,2,1,0:T(2,128)S(1)} %get-tuple-element.8.edge_ref, f32[16,128]{1,0:T(8,128)S(1)} %get-tuple-element.9.strip_ref, ...), custom_call_target="tpu_custom_call" | custom-call | tf_op jit(solution)/shard_map/nest/pallas_call | solution.py:557
  48.2 9.9 %parent.1 = f32[8,3,16,4096]{3,2,1,0:T(8,128)} custom-call(s32[8,2]{1,0:T(8,128)S(1)} %copy.7.off_ref, s32[1]{0:T(128)} %bitcast.band_ref, f32[8,3,16,4096]{3,2,1,0:T(8,128)} %par_ref.3, f32[2,8,2,4096]{3,2,1,0:T(2,128)S(1)} %get-tuple-element.11.halo_ref, f32[8,3,16,128]{3,2,1,0:T(8,128)S(1)} %get-tuple-element.12.patch_ref), custom_call_target="tpu_custom_call" | custom-call | tf_op jit(solution)/shard_map/parent/pallas_call | solution.py:597
  58.0 0.9 %copy.9 = f32[8,3,24,384]{3,2,1,0:T(8,128)} copy(f32[8,3,24,384]{3,2,1,0:T(8,128)S(1)} %get-tuple-element.17) | data formatting | bytes 1769472
Async XLA Ops:
  0.6 8.8 %copy-start = (f32[8,3,24,384]{3,2,1,0:T(8,128)S(1)}, f32[8,3,24,384]{3,2,1,0:T(8,128)}, u32[]{:S(2)}) copy-start(f32[8,3,24,384]{3,2,1,0:T(8,128)} %nest_ref.1) | copy-start | bytes 2654212

commit v3 on v2

--- a/solution.py
+++ b/solution.py
@@ -17,7 +17,6 @@
 keep = 1.0 - friction
 highest = lax.Precision.HIGHEST
 LANES = 128
-HALO = 8
 
 
 def lane_roll(x, shift):
@@ -128,11 +127,13 @@
     nest_out,
     patch,
     halo,
-    ext,
+    given,
+    taken,
+    known,
     strips,
     endbuf,
     cols,
-    side,
+    sides,
     ghost,
     acc,
     fine,
@@ -174,36 +175,27 @@
         return 0
 
     lax.fori_loop(1, bands, greet, 0)
-    own = pltpu.make_async_copy(nest_ref, ext.at[:, :, pl.ds(HALO, nrows), :], local_sem)
+    own = pltpu.make_async_copy(nest_ref, nest_out, local_sem)
     own.start()
     pl.semaphore_wait(barrier, bands - 1)
 
-    reach = 2 * NSTEPS
-
-    def nest_down(mem, to):
+    def nest_copy(step, way, mem, to):
         return remote(
-            nest_ref.at[mem, :, pl.ds(nrows - reach, reach), :],
-            ext.at[mem, :, pl.ds(HALO - reach, reach), :],
-            nest_send.at[0, mem],
-            nest_recv.at[0, mem],
+            given.at[step, way, mem], taken.at[step, way, mem], nest_send.at[step, way, mem], nest_recv.at[step, way, mem], to
+        )
+
+    part = edge_ref.shape[3] // 2
+
+    def edge_copy(piece, way, mem, to):
+        place = pl.ds(piece * part, part)
+        return remote(
+            edge_ref.at[way, mem, :, place],
+            halo.at[way, mem, :, place],
+            edge_send.at[piece, way, mem],
+            edge_recv.at[piece, way, mem],
             to,
         )
 
-    def nest_up(mem, to):
-        return remote(
-            nest_ref.at[mem, :, pl.ds(0, reach), :],
-            ext.at[mem, :, pl.ds(HALO + nrows, reach), :],
-            nest_send.at[1, mem],
-            nest_recv.at[1, mem],
-            to,
-        )
-
-    def edge_down(to):
-        return remote(edge_ref.at[1], halo.at[0], edge_send.at[0], edge_recv.at[0], to)
-
-    def edge_up(to):
-        return remote(edge_ref.at[0], halo.at[1], edge_send.at[1], edge_recv.at[1], to)
-
     def strip_copy(slot, to, index):
         return remote(strip_ref, strips.at[pl.ds(pl.multiple_of((slot + 1) * prows, prows), prows), :], strip_send.at[index], strip_recv.at[slot], to)
 
@@ -229,26 +221,32 @@
     def _():
         end_copy(1, bands - 1 - me, bands - 1).start()
 
-    def send_nest(mem, _):
+    def send_up_down(copy, a, mem):
         @pl.when(jnp.logical_not(first))
         def _():
-            nest_up(mem, me - 1).start()
+            copy(a, 0, mem, me - 1).start()
 
         @pl.when(jnp.logical_not(last))
         def _():
-            nest_down(mem, me + 1).start()
-
-        return 0
-
-    lax.fori_loop(0, members, send_nest, 0)
-
-    @pl.when(jnp.logical_not(first))
-    def _():
-        edge_up(me - 1).start()
-
-    @pl.when(jnp.logical_not(last))
-    def _():
-        edge_down(me + 1).start()
+            copy(a, 1, mem, me + 1).start()
+
+    def await_up_down(copy, a, mem):
+        @pl.when(jnp.logical_not(last))
+        def _():
+            copy(a, 0, mem, me).wait_recv()
+
+        @pl.when(jnp.logical_not(first))
+        def _():
+            copy(a, 1, mem, me).wait_recv()
+
+    def sent_up_down(copy, a, mem):
+        @pl.when(jnp.logical_not(first))
+        def _():
+            copy(a, 0, mem, me).wait_send()
+
+        @pl.when(jnp.logical_not(last))
+        def _():
+            copy(a, 1, mem, me).wait_send()
 
     pad = strips.shape[0] - (bands + 1) * prows
     strips[pl.ds(0, prows), :] = jnp.zeros((prows, LANES), jnp.float32)
@@ -268,21 +266,18 @@
         k = iota((ends_lane, nwidth), 0) - 3
         fine[...] = (jnp.where(k == q, 3 - t, 0) + jnp.where(k == q + 1, t, 0)).astype(jnp.float32).astype(jnp.bfloat16)
 
-    erows = nrows + 2 * HALO
-    e = iota((erows, prows), 0)
+    e = iota((nrows, prows), 0) + 2
     q, t = e // 3, e % 3
-    k = iota((erows, prows), 1)
+    k = iota((nrows, prows), 1)
     weights = jnp.where(k == q, (3 - t).astype(jnp.float32) / 3.0, 0.0) + jnp.where(
         k == q + 1, t.astype(jnp.float32) / 3.0, 0.0
     )
     thin = jnp.where(iota((nwidth, span), 0) // 3 == iota((nwidth, span), 1), 1.0, 0.0).astype(jnp.bfloat16)
-    row = iota((erows, nwidth), 0)
-    col = iota((erows, nwidth), 1)
-    is_ghost = jnp.logical_or(
-        jnp.logical_and(row == HALO - 1, first), jnp.logical_and(row == HALO + nrows, last)
-    )
+    row = iota((nrows, nwidth), 0)
+    col = iota((nrows, nwidth), 1)
     at_west, at_east = col == 0, col == nwidth - 1
-    lanes = iota((erows, LANES), 1)
+    at_top, at_bottom = row == 0, row == nrows - 1
+    lanes = iota((nrows, LANES), 1)
 
     def recv_strip(j, _):
         strip_copy(lax.rem(me + j, bands), me, j).wait_recv()
@@ -298,10 +293,37 @@
     cols[...] = jnp.where(lane < 64, height, g - half * (row_roll(turn, -1) - row_roll(turn, 1)))
     picked = jnp.zeros((prows, LANES), jnp.float32)
     for mem in range(members):
-        begin = off_ref[mem, 0] + (me * tile - 3 + prows)
+        begin = off_ref[mem, 0] + (me * tile - 1 + prows)
         picked = jnp.where(lane % 32 // 2 == mem, cols[pl.ds(begin, prows), :], picked)
-    side[...] = jnp.dot(weights, picked, precision=highest, preferred_element_type=jnp.float32)
-
+    side = jnp.dot(weights, picked, precision=highest, preferred_element_type=jnp.float32)
+    for mem in range(members):
+        for f in range(2):
+            for s in range(2):
+                k = 32 * f + s + 2 * mem
+                sides[mem, 2 * f + s] = jnp.broadcast_to(side[:, k : k + 1], (nrows, LANES))
+    own.wait()
+
+    def ddx(x, f, mem):
+        west, east = [jnp.concatenate([sides[mem, 2 * f + s]] * (nwidth // LANES), axis=-1) for s in range(2)]
+        return jnp.where(at_east, east, lane_roll(x, -1)) - jnp.where(at_west, west, lane_roll(x, 1))
+
+    def ddy(x, above, below):
+        return jnp.where(at_bottom, below, row_roll(x, -1)) - jnp.where(at_top, above, row_roll(x, 1))
+
+    def give(step, mem, h, z, m):
+        q = h - half * ddx(z, 1, mem)
+        known[mem] = q
+        given[step, 0, mem, 0:1] = m[0:1]
+        given[step, 0, mem, 1:2] = q[0:1] - half * m[1:2]
+        given[step, 1, mem, 0:1] = m[nrows - 1 : nrows]
+        given[step, 1, mem, 1:2] = q[nrows - 1 : nrows] + half * m[nrows - 2 : nrows - 1]
+        send_up_down(nest_copy, step, mem)
+
+    def give_first(mem, _):
+        give(0, mem, nest_out[mem, 0], nest_out[mem, 1], nest_out[mem, 2])
+        return 0
+
+    lax.fori_loop(0, members, give_first, 0)
 
     def add_end(k, _):
         @pl.when(k > 0)
@@ -325,8 +347,6 @@
         lax.fori_loop(0, top_senders, add_end, 0)
         rows_in = acc[...].reshape(3 * members, ends_lane)
         ghost[...] = (exact_dot(rows_in, fine[...]) * (1.0 / 3.0)).reshape(3, members, nwidth)
-
-    own.wait()
 
     turn_of = lax.rem(group, per)
 
@@ -339,40 +359,27 @@
             to,
         )
 
-    def one_member(mem, _):
-        @pl.when(jnp.logical_not(first))
-        def _():
-            nest_down(mem, me).wait_recv()
-
-        @pl.when(jnp.logical_not(last))
-        def _():
-            nest_up(mem, me).wait_recv()
-
-        def side_of(f, s):
-            return jnp.sum(jnp.where(lanes == 32 * f + s + 2 * mem, side[...], 0.0), axis=1, keepdims=True)
-
-        sides = [[side_of(f, s) for s in range(2)] for f in range(2)]
-        ends = [ghost[f, pl.ds(mem, 1), :] for f in range(3)]
-
-        def ddx(x, f):
-            left = jnp.where(at_west, sides[f][0], lane_roll(x, 1))
-            right = jnp.where(at_east, sides[f][1], lane_roll(x, -1))
-            return right - left
-
-        def ddy(x):
-            return row_roll(x, -1) - row_roll(x, 1)
-
-        def bound(x, f):
-            return jnp.where(is_ghost, ends[f], x)
-
-        h, z, m = ext[mem, 0], bound(ext[mem, 1], 1), bound(ext[mem, 2], 2)
-        for _ in range(NSTEPS):
-            h = bound(h - half * (ddx(z, 1) + ddy(m)), 0)
-            z, m = (
-                bound(keep * z - half * ddx(h, 0) + rotation * m, 1),
-                bound(keep * m - half * ddy(h) - rotation * z, 2),
-            )
-        inner = [x[HALO : HALO + nrows] for x in (h, z, m)]
+    def one_member(step, mem, _):
+        if step < 2:
+            send_up_down(edge_copy, step, mem)
+        await_up_down(nest_copy, step, mem)
+        z, m = nest_out[mem, 1], nest_out[mem, 2]
+        h_ghost, m_ghost = ghost[0, pl.ds(mem, 1), :], ghost[2, pl.ds(mem, 1), :]
+        m_above = jnp.where(first, m_ghost, taken[step, 1, mem, 0:1])
+        h_above = jnp.where(first, h_ghost, taken[step, 1, mem, 1:2] - half * m[0:1])
+        m_below = jnp.where(last, m_ghost, taken[step, 0, mem, 0:1])
+        h_below = jnp.where(last, h_ghost, taken[step, 0, mem, 1:2] + half * m[nrows - 1 : nrows])
+        h = known[mem] - half * ddy(m, m_above, m_below)
+        z, m = (
+            keep * z - half * ddx(h, 0, mem) + rotation * m,
+            keep * m - half * ddy(h, h_above, h_below) - rotation * z,
+        )
+        if step < NSTEPS - 1:
+            give(step + 1, mem, h, z, m)
+            nest_out[mem, 1] = z
+            nest_out[mem, 2] = m
+            return 0
+        inner = (h, z, m)
         for f, x in enumerate(inner):
             nest_out[mem, f] = x
         sums = exact_dot(jnp.concatenate(inner, axis=0), thin)
@@ -393,7 +400,8 @@
 
         return 0
 
-    lax.fori_loop(0, members, one_member, 0)
+    for step in range(NSTEPS):
+        lax.fori_loop(0, members, functools.partial(one_member, step), 0)
     is_mid = lax.rem(me, per) == turn_of
     mine = me // per
 
@@ -433,16 +441,6 @@
 
     lax.fori_loop(0, members, recv_patch, 0)
 
-    @pl.when(jnp.logical_not(first))
-    def _():
-        edge_down(me).wait_recv()
-        edge_up(me).wait_send()
-
-    @pl.when(jnp.logical_not(last))
-    def _():
-        edge_up(me).wait_recv()
-        edge_down(me).wait_send()
-
     @pl.when(sends_top)
     def _():
         end_copy(0, me, 0).wait_send()
@@ -458,13 +456,11 @@
     lax.fori_loop(1, bands, sent_strip, 0)
 
     def sent_mid(mem, _):
-        @pl.when(jnp.logical_not(first))
-        def _():
-            nest_up(mem, me).wait_send()
-
-        @pl.when(jnp.logical_not(last))
-        def _():
-            nest_down(mem, me).wait_send()
+        for piece in range(2):
+            await_up_down(edge_copy, piece, mem)
+            sent_up_down(edge_copy, piece, mem)
+        for step in range(NSTEPS):
+            sent_up_down(nest_copy, step, mem)
 
         @pl.when(per * mem + turn_of != me)
         def _():
@@ -497,10 +493,10 @@
         down = jnp.where(row == rows - 1, below, row_roll(x, -1))
         return down - up
 
-    m_above = jnp.where(first, 0.0, halo_ref[0, 0, 0:1, :])
-    m_below = jnp.where(last, 0.0, halo_ref[1, 0, 0:1, :])
-    h_above = jnp.where(first, 0.0, halo_ref[0, 0, 1:2, :] - half * m[0:1])
-    h_below = jnp.where(last, 0.0, halo_ref[1, 0, 1:2, :] + half * m[rows - 1 : rows])
+    m_above = jnp.where(first, 0.0, halo_ref[1, 0, 0:1, :])
+    m_below = jnp.where(last, 0.0, halo_ref[0, 0, 0:1, :])
+    h_above = jnp.where(first, 0.0, halo_ref[1, 0, 1:2, :] - half * m[0:1])
+    h_below = jnp.where(last, 0.0, halo_ref[0, 0, 1:2, :] + half * m[rows - 1 : rows])
     h1 = h - courant * dx(z) - half * ddy(m, m_above, m_below)
     out_ref[0, 0] = h1
     out_ref[0, 1] = keep * z - courant * dx(h1) + rotation * m
@@ -564,11 +560,13 @@
         in_specs=[pl.BlockSpec(memory_space=pltpu.SMEM), hbm, hbm, vmem, vmem],
         out_specs=(vmem, vmem, hbm),
         scratch_shapes=[
-            pltpu.VMEM((members, 3, nrows + 2 * HALO, nwidth), f32),
+            pltpu.VMEM((NSTEPS, 2, members, 2, nwidth), f32),
+            pltpu.VMEM((NSTEPS, 2, members, 2, nwidth), f32),
+            pltpu.VMEM((members, nrows, nwidth), f32),
             pltpu.VMEM(((bands + 2) * prows, LANES), f32),
             pltpu.VMEM((senders, 3, members, span + LANES), f32),
             pltpu.VMEM(((bands + 2) * prows, LANES), f32),
-            pltpu.VMEM((nrows + 2 * HALO, LANES), f32),
+            pltpu.VMEM((members, 4, nrows, LANES), f32),
             pltpu.VMEM((3, members, nwidth), f32),
             pltpu.VMEM((3, members, span + LANES), f32),
             pltpu.VMEM((span + LANES, nwidth), jnp.bfloat16),
@@ -576,10 +574,10 @@
             pltpu.VMEM((members, span // LANES, 3, tile, LANES), f32),
             pltpu.VMEM((span // LANES, 3, bands * tile + 2 * prows, LANES), f32),
             pltpu.VMEM((bands, 3, prows, span), f32),
-            dma((2, members)),
-            dma((2, members)),
-            dma((2,)),
-            dma((2,)),
+            dma((NSTEPS, 2, members)),
+            dma((NSTEPS, 2, members)),
+            dma((2, 2, members)),
+            dma((2, 2, members)),
             dma((bands,)),
             dma((bands,)),
             dma((2,)),

time: 59.4 us -> 64.4 us (1.084)
  Pallas kernels: 56.5 us -> 61.5 us
    pallas_call x1, Pallas kernels: 38.8 us -> 43.8 us  [per_device(): pl.pallas_call(functools.partial(nest_kernel, bands, span), out_shape=(sh...]
where the time goes in v3:
time: 64.4 us; the launch traced here: 63.9 us
  Pallas kernels  61.5 us (95%)
  local copies, waits for them, and re-layouts  1.75 us (3%)
  between operations  0.67 us (1%)
    pallas_call x1, Pallas kernels, per_device(): pl.pallas_call(functools.partial(nest_kernel, bands, span), out_shape=(sh...  43.8 us
    pallas_call x1, Pallas kernels, per_device(): pl.pallas_call(functools.partial(parent_kernel, span, bands), out_shape=s...  9.85 us
    pallas_call x1, Pallas kernels, per_device(): pl.pallas_call(functools.partial(gather_kernel, span, bands), out_shape=(...  7.92 us
    unnamed x4, local copies, waits for them, and re-layouts  1.75 us

profile of v3, /device:TPU:0, one launch (start us, length us, event | category | flops | bytes accessed | tf_op | source)
XLA Modules:
  0.0 63.9 jit_solution(15201930327281192459)
XLA Ops:
  0.6 0.0 copy-start
  0.6 0.8 %copy.7.off_ref = s32[8,2]{1,0:T(8,128)S(1)} copy(s32[8,2]{0,1:T(2,128)} %param.5) | data formatting | bytes 128 | tf_op args[2]
  1.5 7.9 %gather.1 = (f32[2,8,2,4096]{3,2,1,0:T(2,128)S(1)}, f32[16,128]{1,0:T(8,128)S(1)}, f32[2,3,8,256]{3,2,1,0:T(8,128)S(1)}) custom-call(s32[8,2]{1,0:T(8,128)S(1)} %copy.7.off_ref, s32[1]{0:T(128)} %bitcast.band_ref, f32[8,3,16,4096]{3,2,1,0:T(8,128)} %par_ref.3), custom_call_target="tpu_custom_call" | custom-call | tf_op jit(solution)/shard_map/gather/pallas_call | solution.py:528
  9.4 0.0 copy-done
  9.4 43.8 %nest.1 = (f32[8,3,24,384]{3,2,1,0:T(8,128)S(1)}, f32[8,3,16,128]{3,2,1,0:T(8,128)S(1)}, f32[2,8,2,4096]{3,2,1,0:T(2,128)S(1)}) custom-call(s32[8,2]{1,0:T(8,128)S(1)} %copy.7.off_ref, f32[8,3,24,384]{3,2,1,0:T(8,128)S(1)} %copy-done, f32[2,8,2,4096]{3,2,1,0:T(2,128)S(1)} %get-tuple-element.8.edge_ref, f32[16,128]{1,0:T(8,128)S(1)} %get-tuple-element.9.strip_ref, ...), custom_call_target="tpu_custom_call" | custom-call | tf_op jit(solution)/shard_map/nest/pallas_call | solution.py:553
  53.2 9.9 %parent.1 = f32[8,3,16,4096]{3,2,1,0:T(8,128)} custom-call(s32[8,2]{1,0:T(8,128)S(1)} %copy.7.off_ref, s32[1]{0:T(128)} %bitcast.band_ref, f32[8,3,16,4096]{3,2,1,0:T(8,128)} %par_ref.3, f32[2,8,2,4096]{3,2,1,0:T(2,128)S(1)} %get-tuple-element.11.halo_ref, f32[8,3,16,128]{3,2,1,0:T(8,128)S(1)} %get-tuple-element.12.patch_ref), custom_call_target="tpu_custom_call" | custom-call | tf_op jit(solution)/shard_map/parent/pallas_call | solution.py:595
  63.0 0.9 %copy.9 = f32[8,3,24,384]{3,2,1,0:T(8,128)} copy(f32[8,3,24,384]{3,2,1,0:T(8,128)S(1)} %get-tuple-element.17) | data formatting | bytes 1769472
Async XLA Ops:
  0.6 8.8 %copy-start = (f32[8,3,24,384]{3,2,1,0:T(8,128)S(1)}, f32[8,3,24,384]{3,2,1,0:T(8,128)}, u32[]{:S(2)}) copy-start(f32[8,3,24,384]{3,2,1,0:T(8,128)} %nest_ref.1) | copy-start | bytes 2654212

commit v4 on v2

--- a/solution.py
+++ b/solution.py
@@ -49,32 +49,34 @@
     return sum(jnp.dot(part, weights, preferred_element_type=jnp.float32) for part in split(x))
 
 
-def gather_kernel(span, bands, off_ref, band_ref, par_ref, edge_ref, strip_ref, ends_ref):
-    mem = pl.program_id(0)
+def edge_rows(mem, par_ref, edge_ref):
+    rows = par_ref.shape[2]
+    z_top, z_bot = par_ref[mem, 1, 0:1, :], par_ref[mem, 1, rows - 1 : rows, :]
+    m_top, m_bot = par_ref[mem, 2, 0:1, :], par_ref[mem, 2, rows - 1 : rows, :]
+    edge_ref[0, mem, 0:1, :] = m_top
+    edge_ref[0, mem, 1:2, :] = par_ref[mem, 0, 0:1, :] - courant * dx(z_top) - half * par_ref[mem, 2, 1:2, :]
+    edge_ref[1, mem, 0:1, :] = m_bot
+    edge_ref[1, mem, 1:2, :] = (
+        par_ref[mem, 0, rows - 1 : rows, :] - courant * dx(z_bot) + half * par_ref[mem, 2, rows - 2 : rows - 1, :]
+    )
+
+
+def window_shares(mem, span, row0, col0, band, par_ref, ends_ref):
     rows, width = par_ref.shape[2], par_ref.shape[3]
-    row0, col0 = off_ref[mem, 0], off_ref[mem, 1]
-    band = band_ref[0]
-
-    z_top, z_bot = par_ref[0, 1, 0:1, :], par_ref[0, 1, rows - 1 : rows, :]
-    m_top, m_bot = par_ref[0, 2, 0:1, :], par_ref[0, 2, rows - 1 : rows, :]
-    edge_ref[0, 0, 0:1, :] = m_top
-    edge_ref[0, 0, 1:2, :] = par_ref[0, 0, 0:1, :] - courant * dx(z_top) - half * par_ref[0, 2, 1:2, :]
-    edge_ref[1, 0, 0:1, :] = m_bot
-    edge_ref[1, 0, 1:2, :] = (
-        par_ref[0, 0, rows - 1 : rows, :] - courant * dx(z_bot) + half * par_ref[0, 2, rows - 2 : rows - 1, :]
-    )
-
     blocks = width // LANES
     count = span // LANES + 2
     first = lax.rem(col0 - 4 + width, width)
-    block0 = first // LANES
+    block0 = lax.div(first, LANES)
     shift = first - block0 * LANES
-    parts = [
-        par_ref[0, :, :, pl.ds(pl.multiple_of(lax.rem(block0 + k, blocks) * LANES, LANES), LANES)]
-        for k in range(count)
-    ]
+    wanted = [jnp.zeros((rows, LANES), jnp.int32) + lax.rem(block0 + k, blocks) for k in range(count)]
+    parts = [jnp.zeros((3, rows, LANES), jnp.float32)] * count
+    for place in range(blocks):
+        block = par_ref[mem, :, :, place * LANES : (place + 1) * LANES]
+        parts = [jnp.where((w == place)[None], block, part) for w, part in zip(wanted, parts)]
     wide = jnp.concatenate(parts, axis=-1).reshape(3 * rows, count * LANES)
-    wide = pltpu.roll(wide, lax.rem(count * LANES - shift, count * LANES), 1)
+    amount = jnp.zeros(wide.shape, jnp.int32) + shift
+    for bit in (64, 32, 16, 8, 4, 2, 1):
+        wide = jnp.where((amount & bit) != 0, lane_roll(wide, -bit), wide)
     wide = wide[:, : span + LANES].reshape(3, rows, span + LANES)
     h, z, m = wide[0], wide[1], wide[2]
     a = h - courant * dx(z)
@@ -91,12 +93,6 @@
             value = jnp.sum(field * weight, axis=1, keepdims=True)
             total = total + jnp.where(slot == q * 16 + s + 2 * mem, value, 0.0)
 
-    @pl.when(mem == 0)
-    def _():
-        strip_ref[...] = jnp.zeros_like(strip_ref)
-
-    strip_ref[...] += total
-
     row = iota(shape, 0) + band * rows
     for end in range(2):
         near = row0 - 1 if end == 0 else row0 + span - 1
@@ -115,6 +111,7 @@
         m1 = jnp.sum(wr * cc + ur * a + vr * m, axis=0, keepdims=True)
         for f, value in enumerate((h1, z1, m1)):
             ends_ref[end, f, pl.ds(mem, 1), :] = value
+    return total
 
 
 def nest_kernel(
@@ -122,12 +119,14 @@
     span,
     off_ref,
     nest_ref,
+    parent_ref,
+    nest_out,
+    patch,
+    halo,
+    par_ref,
     edge_ref,
     strip_ref,
     ends_ref,
-    nest_out,
-    patch,
-    halo,
     ext,
     strips,
     endbuf,
@@ -153,6 +152,7 @@
     out_send,
     out_recv,
     local_sem,
+    parent_sem,
 ):
     me = lax.axis_index("band")
     group = lax.axis_index("member")
@@ -175,6 +175,8 @@
 
     lax.fori_loop(1, bands, greet, 0)
     own = pltpu.make_async_copy(nest_ref, ext.at[:, :, pl.ds(HALO, nrows), :], local_sem)
+    load = pltpu.make_async_copy(parent_ref, par_ref, parent_sem)
+    load.start()
     own.start()
     pl.semaphore_wait(barrier, bands - 1)
 
@@ -212,6 +214,22 @@
 
     first, last = me == 0, me == bands - 1
 
+    def gather(mem, _):
+        @pl.when(jnp.logical_not(first))
+        def _():
+            nest_up(mem, me - 1).start()
+
+        @pl.when(jnp.logical_not(last))
+        def _():
+            nest_down(mem, me + 1).start()
+
+        strip_ref[...] += window_shares(mem, span, off_ref[mem, 0], off_ref[mem, 1], me, par_ref, ends_ref)
+        return 0
+
+    strip_ref[...] = jnp.zeros_like(strip_ref)
+    load.wait()
+    lax.fori_loop(0, members, gather, 0)
+
     def send_strip(j, _):
         strip_copy(me, lax.rem(me + j, bands), j).start()
         return 0
@@ -229,18 +247,11 @@
     def _():
         end_copy(1, bands - 1 - me, bands - 1).start()
 
-    def send_nest(mem, _):
-        @pl.when(jnp.logical_not(first))
-        def _():
-            nest_up(mem, me - 1).start()
-
-        @pl.when(jnp.logical_not(last))
-        def _():
-            nest_down(mem, me + 1).start()
-
-        return 0
-
-    lax.fori_loop(0, members, send_nest, 0)
+    def send_edges(mem, _):
+        edge_rows(mem, par_ref, edge_ref)
+        return 0
+
+    lax.fori_loop(0, members, send_edges, 0)
 
     @pl.when(jnp.logical_not(first))
     def _():
@@ -489,22 +500,35 @@
     row0, col0 = off_ref[mem, 0], off_ref[mem, 1]
     band = band_ref[0]
     first, last = band == 0, band == bands - 1
-    h, z, m = par_ref[0, 0], par_ref[0, 1], par_ref[0, 2]
-    row = iota(h.shape, 0)
+    piece = 4 * LANES
+    row = iota((rows, piece + 2 * LANES), 0)
+    at_top, at_bottom = row == 0, row == rows - 1
 
     def ddy(x, above, below):
-        up = jnp.where(row == 0, above, row_roll(x, 1))
-        down = jnp.where(row == rows - 1, below, row_roll(x, -1))
-        return down - up
-
-    m_above = jnp.where(first, 0.0, halo_ref[0, 0, 0:1, :])
-    m_below = jnp.where(last, 0.0, halo_ref[1, 0, 0:1, :])
-    h_above = jnp.where(first, 0.0, halo_ref[0, 0, 1:2, :] - half * m[0:1])
-    h_below = jnp.where(last, 0.0, halo_ref[1, 0, 1:2, :] + half * m[rows - 1 : rows])
-    h1 = h - courant * dx(z) - half * ddy(m, m_above, m_below)
-    out_ref[0, 0] = h1
-    out_ref[0, 1] = keep * z - courant * dx(h1) + rotation * m
-    out_ref[0, 2] = keep * m - half * ddy(h1, h_above, h_below) - rotation * z
+        return jnp.where(at_bottom, below, row_roll(x, -1)) - jnp.where(at_top, above, row_roll(x, 1))
+
+    for begin in range(0, width, piece):
+
+        def cut(ref, *index):
+            left, right = (begin - LANES) % width, (begin + piece) % width
+            if left + piece + 2 * LANES == right + LANES:
+                return ref[(*index, slice(left, right + LANES))]
+            parts = (left, left + LANES), (begin, begin + piece), (right, right + LANES)
+            return jnp.concatenate([ref[(*index, slice(*part))] for part in parts], axis=-1)
+
+        every = slice(None)
+        h, z, m = [cut(par_ref, 0, f, every) for f in range(3)]
+        above = cut(halo_ref, 0, 0, every)
+        below = cut(halo_ref, 1, 0, every)
+        m_above = jnp.where(first, 0.0, above[0:1])
+        m_below = jnp.where(last, 0.0, below[0:1])
+        h_above = jnp.where(first, 0.0, above[1:2] - half * m[0:1])
+        h_below = jnp.where(last, 0.0, below[1:2] + half * m[rows - 1 : rows])
+        h1 = h - half * (lane_roll(z, -1) - lane_roll(z, 1) + ddy(m, m_above, m_below))
+        z1 = keep * z - half * (lane_roll(h1, -1) - lane_roll(h1, 1)) + rotation * m
+        m1 = keep * m - half * ddy(h1, h_above, h_below) - rotation * z
+        for f, x in enumerate((h1, z1, m1)):
+            out_ref[0, f, :, begin : begin + piece] = x[:, LANES : LANES + piece]
 
     block0 = col0 // LANES
     shift = col0 - block0 * LANES
@@ -529,27 +553,6 @@
     parent_spec = pl.BlockSpec((1, 3, prows, width), lambda i, *_: (i, 0, 0, 0))
     edge_spec = pl.BlockSpec((2, 1, 2, width), lambda i, *_: (0, i, 0, 0))
 
-    edges, strip, ends = pl.pallas_call(
-        functools.partial(gather_kernel, span, bands),
-        out_shape=(
-            shape((2, members, 2, width), f32),
-            shape((prows, LANES), f32),
-            shape((2, 3, members, span + LANES), f32),
-        ),
-        grid_spec=pltpu.PrefetchScalarGridSpec(
-            num_scalar_prefetch=2,
-            grid=(members,),
-            in_specs=[parent_spec],
-            out_specs=(
-                edge_spec,
-                pl.BlockSpec((prows, LANES), lambda i, *_: (0, 0)),
-                pl.BlockSpec((2, 3, members, span + LANES), lambda i, *_: (0, 0, 0, 0)),
-            ),
-        ),
-        compiler_params=pltpu.CompilerParams(vmem_limit_bytes=limit),
-        name="gather",
-    )(offsets, band, parent_state)
-
     vmem = pl.BlockSpec(memory_space=pltpu.VMEM)
     hbm = pl.BlockSpec(memory_space=pl.ANY)
     dma = pltpu.SemaphoreType.DMA
@@ -561,9 +564,13 @@
             shape((members, 3, prows, span), f32),
             shape((2, members, 2, width), f32),
         ),
-        in_specs=[pl.BlockSpec(memory_space=pltpu.SMEM), hbm, hbm, vmem, vmem],
+        in_specs=[pl.BlockSpec(memory_space=pltpu.SMEM), hbm, hbm],
         out_specs=(vmem, vmem, hbm),
         scratch_shapes=[
+            pltpu.VMEM((members, 3, prows, width), f32),
+            pltpu.VMEM((2, members, 2, width), f32),
+            pltpu.VMEM((prows, LANES), f32),
+            pltpu.VMEM((2, 3, members, span + LANES), f32),
             pltpu.VMEM((members, 3, nrows + 2 * HALO, nwidth), f32),
             pltpu.VMEM(((bands + 2) * prows, LANES), f32),
             pltpu.VMEM((senders, 3, members, span + LANES), f32),
@@ -589,10 +596,11 @@
             dma((bands,)),
             dma((members,)),
             dma,
+            dma,
         ],
         compiler_params=pltpu.CompilerParams(collective_id=0, has_side_effects=True, vmem_limit_bytes=limit),
         name="nest",
-    )(offsets, nest_state, edges, strip, ends)
+    )(offsets, nest_state, parent_state)
 
     parent_out = pl.pallas_call(
         functools.partial(parent_kernel, span, bands),

time: 59.4 us -> 60.5 us (1.019)
  local copies, waits for them, and re-layouts: 1.75 us -> 2.83 us
    pallas_call x1 -> x0, Pallas kernels: 7.92 us -> none  [per_device(): pl.pallas_call(functools.partial(gather_kernel, span, bands), out_shape=(...]
    pallas_call x1, Pallas kernels: 38.8 us -> 45.3 us  [per_device(): pl.pallas_call(functools.partial(nest_kernel, bands, span), out_shape=(sh...]
    pallas_call x1, Pallas kernels: 9.86 us -> 11.4 us  [per_device(): pl.pallas_call(functools.partial(parent_kernel, span, bands), out_shape=s...]
    unnamed x4, local copies, waits for them, and re-layouts: 1.75 us -> 2.83 us
where the time goes in v4:
time: 60.5 us; the launch traced here: 60.2 us
  Pallas kernels  56.7 us (94%)
  local copies, waits for them, and re-layouts  2.83 us (5%)
  between operations  0.64 us (1%)
    pallas_call x1, Pallas kernels, per_device(): pl.pallas_call(functools.partial(nest_kernel, bands, span), out_shape=(sh...  45.3 us
    pallas_call x1, Pallas kernels, per_device(): pl.pallas_call(functools.partial(parent_kernel, span, bands), out_shape=s...  11.4 us
    unnamed x4, local copies, waits for them, and re-layouts  2.83 us

profile of v4, /device:TPU:0, one launch (start us, length us, event | category | flops | bytes accessed | tf_op | source)
XLA Modules:
  0.0 60.2 jit_solution(1265267240110400172)
XLA Ops:
  0.6 0.8 %copy.6.off_ref = s32[8,2]{1,0:T(8,128)S(1)} copy(s32[8,2]{0,1:T(2,128)} %param.5) | data formatting | bytes 128 | tf_op args[2]
  1.4 0.0 copy-start
  1.4 1.2 %copy-done = f32[8,3,24,384]{3,2,1,0:T(8,128)S(1)} copy-done((f32[8,3,24,384]{3,2,1,0:T(8,128)S(1)}, f32[8,3,24,384]{3,2,1,0:T(8,128)}, u32[]{:S(2)}) %copy-start) | copy-done | bytes 884760
  2.6 45.3 %nest.1 = (f32[8,3,24,384]{3,2,1,0:T(8,128)S(1)}, f32[8,3,16,128]{3,2,1,0:T(8,128)S(1)}, f32[2,8,2,4096]{3,2,1,0:T(2,128)S(1)}) custom-call(s32[8,2]{1,0:T(8,128)S(1)} %copy.6.off_ref, f32[8,3,24,384]{3,2,1,0:T(8,128)S(1)} %copy-done, f32[8,3,16,4096]{3,2,1,0:T(8,128)} %par_ref.1), custom_call_target="tpu_custom_call" | custom-call | tf_op jit(solution)/shard_map/nest/pallas_call | solution.py:560
  47.9 11.4 %parent.1 = f32[8,3,16,4096]{3,2,1,0:T(8,128)} custom-call(s32[8,2]{1,0:T(8,128)S(1)} %copy.6.off_ref, s32[1]{0:T(128)} %bitcast.band_ref, f32[8,3,16,4096]{3,2,1,0:T(8,128)} %par_ref.1, f32[2,8,2,4096]{3,2,1,0:T(2,128)S(1)} %get-tuple-element.5.halo_ref, f32[8,3,16,128]{3,2,1,0:T(8,128)S(1)} %get-tuple-element.6.patch_ref), custom_call_target="tpu_custom_call" | custom-call | tf_op jit(solution)/shard_map/parent/pallas_call | solution.py:605
  59.2 0.9 %copy.8 = f32[8,3,24,384]{3,2,1,0:T(8,128)} copy(f32[8,3,24,384]{3,2,1,0:T(8,128)S(1)} %get-tuple-element.11) | data formatting | bytes 1769472
Async XLA Ops:
  1.4 1.2 %copy-start = (f32[8,3,24,384]{3,2,1,0:T(8,128)S(1)}, f32[8,3,24,384]{3,2,1,0:T(8,128)}, u32[]{:S(2)}) copy-start(f32[8,3,24,384]{3,2,1,0:T(8,128)} %nest_ref.1) | copy-start | bytes 2654212

commit v5 on v3

--- a/solution.py
+++ b/solution.py
@@ -48,32 +48,34 @@
     return sum(jnp.dot(part, weights, preferred_element_type=jnp.float32) for part in split(x))
 
 
-def gather_kernel(span, bands, off_ref, band_ref, par_ref, edge_ref, strip_ref, ends_ref):
-    mem = pl.program_id(0)
+def edge_rows(mem, par_ref, edge_ref):
+    rows = par_ref.shape[2]
+    z_top, z_bot = par_ref[mem, 1, 0:1, :], par_ref[mem, 1, rows - 1 : rows, :]
+    m_top, m_bot = par_ref[mem, 2, 0:1, :], par_ref[mem, 2, rows - 1 : rows, :]
+    edge_ref[0, mem, 0:1, :] = m_top
+    edge_ref[0, mem, 1:2, :] = par_ref[mem, 0, 0:1, :] - courant * dx(z_top) - half * par_ref[mem, 2, 1:2, :]
+    edge_ref[1, mem, 0:1, :] = m_bot
+    edge_ref[1, mem, 1:2, :] = (
+        par_ref[mem, 0, rows - 1 : rows, :] - courant * dx(z_bot) + half * par_ref[mem, 2, rows - 2 : rows - 1, :]
+    )
+
+
+def window_shares(mem, span, row0, col0, band, par_ref, ends_ref):
     rows, width = par_ref.shape[2], par_ref.shape[3]
-    row0, col0 = off_ref[mem, 0], off_ref[mem, 1]
-    band = band_ref[0]
-
-    z_top, z_bot = par_ref[0, 1, 0:1, :], par_ref[0, 1, rows - 1 : rows, :]
-    m_top, m_bot = par_ref[0, 2, 0:1, :], par_ref[0, 2, rows - 1 : rows, :]
-    edge_ref[0, 0, 0:1, :] = m_top
-    edge_ref[0, 0, 1:2, :] = par_ref[0, 0, 0:1, :] - courant * dx(z_top) - half * par_ref[0, 2, 1:2, :]
-    edge_ref[1, 0, 0:1, :] = m_bot
-    edge_ref[1, 0, 1:2, :] = (
-        par_ref[0, 0, rows - 1 : rows, :] - courant * dx(z_bot) + half * par_ref[0, 2, rows - 2 : rows - 1, :]
-    )
-
     blocks = width // LANES
     count = span // LANES + 2
     first = lax.rem(col0 - 4 + width, width)
-    block0 = first // LANES
+    block0 = lax.div(first, LANES)
     shift = first - block0 * LANES
-    parts = [
-        par_ref[0, :, :, pl.ds(pl.multiple_of(lax.rem(block0 + k, blocks) * LANES, LANES), LANES)]
-        for k in range(count)
-    ]
+    wanted = [jnp.zeros((rows, LANES), jnp.int32) + lax.rem(block0 + k, blocks) for k in range(count)]
+    parts = [jnp.zeros((3, rows, LANES), jnp.float32)] * count
+    for place in range(blocks):
+        block = par_ref[mem, :, :, place * LANES : (place + 1) * LANES]
+        parts = [jnp.where((w == place)[None], block, part) for w, part in zip(wanted, parts)]
     wide = jnp.concatenate(parts, axis=-1).reshape(3 * rows, count * LANES)
-    wide = pltpu.roll(wide, lax.rem(count * LANES - shift, count * LANES), 1)
+    amount = jnp.zeros(wide.shape, jnp.int32) + shift
+    for bit in (64, 32, 16, 8, 4, 2, 1):
+        wide = jnp.where((amount & bit) != 0, lane_roll(wide, -bit), wide)
     wide = wide[:, : span + LANES].reshape(3, rows, span + LANES)
     h, z, m = wide[0], wide[1], wide[2]
     a = h - courant * dx(z)
@@ -90,12 +92,6 @@
             value = jnp.sum(field * weight, axis=1, keepdims=True)
             total = total + jnp.where(slot == q * 16 + s + 2 * mem, value, 0.0)
 
-    @pl.when(mem == 0)
-    def _():
-        strip_ref[...] = jnp.zeros_like(strip_ref)
-
-    strip_ref[...] += total
-
     row = iota(shape, 0) + band * rows
     for end in range(2):
         near = row0 - 1 if end == 0 else row0 + span - 1
@@ -114,6 +110,7 @@
         m1 = jnp.sum(wr * cc + ur * a + vr * m, axis=0, keepdims=True)
         for f, value in enumerate((h1, z1, m1)):
             ends_ref[end, f, pl.ds(mem, 1), :] = value
+    return total
 
 
 def nest_kernel(
@@ -121,12 +118,14 @@
     span,
     off_ref,
     nest_ref,
+    parent_ref,
+    nest_out,
+    patch,
+    halo,
+    par_ref,
     edge_ref,
     strip_ref,
     ends_ref,
-    nest_out,
-    patch,
-    halo,
     given,
     taken,
     known,
@@ -154,6 +153,7 @@
     out_send,
     out_recv,
     local_sem,
+    parent_sem,
 ):
     me = lax.axis_index("band")
     group = lax.axis_index("member")
@@ -176,6 +176,8 @@
 
     lax.fori_loop(1, bands, greet, 0)
     own = pltpu.make_async_copy(nest_ref, nest_out, local_sem)
+    load = pltpu.make_async_copy(parent_ref, par_ref, parent_sem)
+    load.start()
     own.start()
     pl.semaphore_wait(barrier, bands - 1)
 
@@ -184,16 +186,9 @@
             given.at[step, way, mem], taken.at[step, way, mem], nest_send.at[step, way, mem], nest_recv.at[step, way, mem], to
         )
 
-    part = edge_ref.shape[3] // 2
-
     def edge_copy(piece, way, mem, to):
-        place = pl.ds(piece * part, part)
         return remote(
-            edge_ref.at[way, mem, :, place],
-            halo.at[way, mem, :, place],
-            edge_send.at[piece, way, mem],
-            edge_recv.at[piece, way, mem],
-            to,
+            edge_ref.at[way, mem], halo.at[way, mem], edge_send.at[piece, way, mem], edge_recv.at[piece, way, mem], to
         )
 
     def strip_copy(slot, to, index):
@@ -204,6 +199,43 @@
 
     first, last = me == 0, me == bands - 1
 
+    def send_up_down(copy, a, mem):
+        @pl.when(jnp.logical_not(first))
+        def _():
+            copy(a, 0, mem, me - 1).start()
+
+        @pl.when(jnp.logical_not(last))
+        def _():
+            copy(a, 1, mem, me + 1).start()
+
+    def await_up_down(copy, a, mem):
+        @pl.when(jnp.logical_not(last))
+        def _():
+            copy(a, 0, mem, me).wait_recv()
+
+        @pl.when(jnp.logical_not(first))
+        def _():
+            copy(a, 1, mem, me).wait_recv()
+
+    def sent_up_down(copy, a, mem):
+        @pl.when(jnp.logical_not(first))
+        def _():
+            copy(a, 0, mem, me).wait_send()
+
+        @pl.when(jnp.logical_not(last))
+        def _():
+            copy(a, 1, mem, me).wait_send()
+
+    def gather(mem, _):
+        edge_rows(mem, par_ref, edge_ref)
+        send_up_down(edge_copy, 0, mem)
+        strip_ref[...] += window_shares(mem, span, off_ref[mem, 0], off_ref[mem, 1], me, par_ref, ends_ref)
+        return 0
+
+    strip_ref[...] = jnp.zeros_like(strip_ref)
+    load.wait()
+    lax.fori_loop(0, members, gather, 0)
+
     def send_strip(j, _):
         strip_copy(me, lax.rem(me + j, bands), j).start()
         return 0
@@ -220,33 +252,6 @@
     @pl.when(sends_bottom)
     def _():
         end_copy(1, bands - 1 - me, bands - 1).start()
-
-    def send_up_down(copy, a, mem):
-        @pl.when(jnp.logical_not(first))
-        def _():
-            copy(a, 0, mem, me - 1).start()
-
-        @pl.when(jnp.logical_not(last))
-        def _():
-            copy(a, 1, mem, me + 1).start()
-
-    def await_up_down(copy, a, mem):
-        @pl.when(jnp.logical_not(last))
-        def _():
-            copy(a, 0, mem, me).wait_recv()
-
-        @pl.when(jnp.logical_not(first))
-        def _():
-            copy(a, 1, mem, me).wait_recv()
-
-    def sent_up_down(copy, a, mem):
-        @pl.when(jnp.logical_not(first))
-        def _():
-            copy(a, 0, mem, me).wait_send()
-
-        @pl.when(jnp.logical_not(last))
-        def _():
-            copy(a, 1, mem, me).wait_send()
 
     pad = strips.shape[0] - (bands + 1) * prows
     strips[pl.ds(0, prows), :] = jnp.zeros((prows, LANES), jnp.float32)
@@ -360,8 +365,6 @@
         )
 
     def one_member(step, mem, _):
-        if step < 2:
-            send_up_down(edge_copy, step, mem)
         await_up_down(nest_copy, step, mem)
         z, m = nest_out[mem, 1], nest_out[mem, 2]
         h_ghost, m_ghost = ghost[0, pl.ds(mem, 1), :], ghost[2, pl.ds(mem, 1), :]
@@ -456,9 +459,8 @@
     lax.fori_loop(1, bands, sent_strip, 0)
 
     def sent_mid(mem, _):
-        for piece in range(2):
-            await_up_down(edge_copy, piece, mem)
-            sent_up_down(edge_copy, piece, mem)
+        await_up_down(edge_copy, 0, mem)
+        sent_up_down(edge_copy, 0, mem)
         for step in range(NSTEPS):
             sent_up_down(nest_copy, step, mem)
 
@@ -525,27 +527,6 @@
     parent_spec = pl.BlockSpec((1, 3, prows, width), lambda i, *_: (i, 0, 0, 0))
     edge_spec = pl.BlockSpec((2, 1, 2, width), lambda i, *_: (0, i, 0, 0))
 
-    edges, strip, ends = pl.pallas_call(
-        functools.partial(gather_kernel, span, bands),
-        out_shape=(
-            shape((2, members, 2, width), f32),
-            shape((prows, LANES), f32),
-            shape((2, 3, members, span + LANES), f32),
-        ),
-        grid_spec=pltpu.PrefetchScalarGridSpec(
-            num_scalar_prefetch=2,
-            grid=(members,),
-            in_specs=[parent_spec],
-            out_specs=(
-                edge_spec,
-                pl.BlockSpec((prows, LANES), lambda i, *_: (0, 0)),
-                pl.BlockSpec((2, 3, members, span + LANES), lambda i, *_: (0, 0, 0, 0)),
-            ),
-        ),
-        compiler_params=pltpu.CompilerParams(vmem_limit_bytes=limit),
-        name="gather",
-    )(offsets, band, parent_state)
-
     vmem = pl.BlockSpec(memory_space=pltpu.VMEM)
     hbm = pl.BlockSpec(memory_space=pl.ANY)
     dma = pltpu.SemaphoreType.DMA
@@ -557,9 +538,13 @@
             shape((members, 3, prows, span), f32),
             shape((2, members, 2, width), f32),
         ),
-        in_specs=[pl.BlockSpec(memory_space=pltpu.SMEM), hbm, hbm, vmem, vmem],
+        in_specs=[pl.BlockSpec(memory_space=pltpu.SMEM), hbm, hbm],
         out_specs=(vmem, vmem, hbm),
         scratch_shapes=[
+            pltpu.VMEM((members, 3, prows, width), f32),
+            pltpu.VMEM((2, members, 2, width), f32),
+            pltpu.VMEM((prows, LANES), f32),
+            pltpu.VMEM((2, 3, members, span + LANES), f32),
             pltpu.VMEM((NSTEPS, 2, members, 2, nwidth), f32),
             pltpu.VMEM((NSTEPS, 2, members, 2, nwidth), f32),
             pltpu.VMEM((members, nrows, nwidth), f32),
@@ -576,8 +561,8 @@
             pltpu.VMEM((bands, 3, prows, span), f32),
             dma((NSTEPS, 2, members)),
             dma((NSTEPS, 2, members)),
-            dma((2, 2, members)),
-            dma((2, 2, members)),
+            dma((1, 2, members)),
+            dma((1, 2, members)),
             dma((bands,)),
             dma((bands,)),
             dma((2,)),
@@ -587,10 +572,11 @@
             dma((bands,)),
             dma((members,)),
             dma,
+            dma,
         ],
         compiler_params=pltpu.CompilerParams(collective_id=0, has_side_effects=True, vmem_limit_bytes=limit),
         name="nest",
-    )(offsets, nest_state, edges, strip, ends)
+    )(offsets, nest_state, parent_state)
 
     parent_out = pl.pallas_call(
         functools.partial(parent_kernel, span, bands),

time: 64.4 us -> 62.6 us (0.972)
  Pallas kernels: 61.5 us -> 58.7 us
  local copies, waits for them, and re-layouts: 1.75 us -> 2.83 us
    pallas_call x1 -> x0, Pallas kernels: 7.92 us -> none  [per_device(): pl.pallas_call(functools.partial(gather_kernel, span, bands), out_shape=(...]
    pallas_call x1, Pallas kernels: 43.8 us -> 48.9 us  [per_device(): pl.pallas_call(functools.partial(nest_kernel, bands, span), out_shape=(sh...]
    unnamed x4, local copies, waits for them, and re-layouts: 1.75 us -> 2.83 us
where the time goes in v5:
time: 62.6 us; the launch traced here: 62.2 us
  Pallas kernels  58.7 us (94%)
  local copies, waits for them, and re-layouts  2.83 us (5%)
  between operations  0.64 us (1%)
    pallas_call x1, Pallas kernels, per_device(): pl.pallas_call(functools.partial(nest_kernel, bands, span), out_shape=(sh...  48.9 us
    pallas_call x1, Pallas kernels, per_device(): pl.pallas_call(functools.partial(parent_kernel, span, bands), out_shape=s...  9.86 us
    unnamed x4, local copies, waits for them, and re-layouts  2.83 us

profile of v5, /device:TPU:0, one launch (start us, length us, event | category | flops | bytes accessed | tf_op | source)
XLA Modules:
  0.0 62.2 jit_solution(5163126634575136059)
XLA Ops:
  0.6 0.8 %copy.6.off_ref = s32[8,2]{1,0:T(8,128)S(1)} copy(s32[8,2]{0,1:T(2,128)} %param.5) | data formatting | bytes 128 | tf_op args[2]
  1.4 0.0 copy-start
  1.4 1.2 %copy-done = f32[8,3,24,384]{3,2,1,0:T(8,128)S(1)} copy-done((f32[8,3,24,384]{3,2,1,0:T(8,128)S(1)}, f32[8,3,24,384]{3,2,1,0:T(8,128)}, u32[]{:S(2)}) %copy-start) | copy-done | bytes 884760
  2.6 48.9 %nest.1 = (f32[8,3,24,384]{3,2,1,0:T(8,128)S(1)}, f32[8,3,16,128]{3,2,1,0:T(8,128)S(1)}, f32[2,8,2,4096]{3,2,1,0:T(2,128)S(1)}) custom-call(s32[8,2]{1,0:T(8,128)S(1)} %copy.6.off_ref, f32[8,3,24,384]{3,2,1,0:T(8,128)S(1)} %copy-done, f32[8,3,16,4096]{3,2,1,0:T(8,128)} %par_ref.1), custom_call_target="tpu_custom_call" | custom-call | tf_op jit(solution)/shard_map/nest/pallas_call | solution.py:534
  51.4 9.9 %parent.1 = f32[8,3,16,4096]{3,2,1,0:T(8,128)} custom-call(s32[8,2]{1,0:T(8,128)S(1)} %copy.6.off_ref, s32[1]{0:T(128)} %bitcast.band_ref, f32[8,3,16,4096]{3,2,1,0:T(8,128)} %par_ref.1, f32[2,8,2,4096]{3,2,1,0:T(2,128)S(1)} %get-tuple-element.5.halo_ref, f32[8,3,16,128]{3,2,1,0:T(8,128)S(1)} %get-tuple-element.6.patch_ref), custom_call_target="tpu_custom_call" | custom-call | tf_op jit(solution)/shard_map/parent/pallas_call | solution.py:581
  61.3 0.9 %copy.8 = f32[8,3,24,384]{3,2,1,0:T(8,128)} copy(f32[8,3,24,384]{3,2,1,0:T(8,128)S(1)} %get-tuple-element.11) | data formatting | bytes 1769472
Async XLA Ops:
  1.4 1.2 %copy-start = (f32[8,3,24,384]{3,2,1,0:T(8,128)S(1)}, f32[8,3,24,384]{3,2,1,0:T(8,128)}, u32[]{:S(2)}) copy-start(f32[8,3,24,384]{3,2,1,0:T(8,128)} %nest_ref.1) | copy-start | bytes 2654212

commit v6 on v4

--- a/solution.py
+++ b/solution.py
@@ -46,7 +46,10 @@
 
 
 def exact_dot(x, weights):
-    return sum(jnp.dot(part, weights, preferred_element_type=jnp.float32) for part in split(x))
+    count = x.shape[0]
+    parts = jnp.concatenate([part.astype(jnp.float32) for part in split(x)], axis=0).astype(jnp.bfloat16)
+    out = jnp.dot(parts, weights, preferred_element_type=jnp.float32)
+    return out[:count] + out[count : 2 * count] + out[2 * count :]
 
 
 def edge_rows(mem, par_ref, edge_ref):
@@ -223,7 +226,7 @@
         def _():
             nest_down(mem, me + 1).start()
 
-        strip_ref[...] += window_shares(mem, span, off_ref[mem, 0], off_ref[mem, 1], me, par_ref, ends_ref)
+        strip_ref[...] += window_shares(mem, span, off_ref[0, mem], off_ref[1, mem], me, par_ref, ends_ref)
         return 0
 
     strip_ref[...] = jnp.zeros_like(strip_ref)
@@ -309,7 +312,7 @@
     cols[...] = jnp.where(lane < 64, height, g - half * (row_roll(turn, -1) - row_roll(turn, 1)))
     picked = jnp.zeros((prows, LANES), jnp.float32)
     for mem in range(members):
-        begin = off_ref[mem, 0] + (me * tile - 3 + prows)
+        begin = off_ref[0, mem] + (me * tile - 3 + prows)
         picked = jnp.where(lane % 32 // 2 == mem, cols[pl.ds(begin, prows), :], picked)
     side[...] = jnp.dot(weights, picked, precision=highest, preferred_element_type=jnp.float32)
 
@@ -350,15 +353,7 @@
             to,
         )
 
-    def one_member(mem, _):
-        @pl.when(jnp.logical_not(first))
-        def _():
-            nest_down(mem, me).wait_recv()
-
-        @pl.when(jnp.logical_not(last))
-        def _():
-            nest_up(mem, me).wait_recv()
-
+    def one_member(mem, slot):
         def side_of(f, s):
             return jnp.sum(jnp.where(lanes == 32 * f + s + 2 * mem, side[...], 0.0), axis=1, keepdims=True)
 
@@ -383,28 +378,49 @@
                 bound(keep * z - half * ddx(h, 0) + rotation * m, 1),
                 bound(keep * m - half * ddy(h) - rotation * z, 2),
             )
-        inner = [x[HALO : HALO + nrows] for x in (h, z, m)]
-        for f, x in enumerate(inner):
+        lines = []
+        for f, x in enumerate((h, z, m)):
+            x = x[HALO : HALO + nrows]
             nest_out[mem, f] = x
-        sums = exact_dot(jnp.concatenate(inner, axis=0), thin)
-        for k in range(span // LANES):
-            thinned[k] = sums[:, k * LANES : (k + 1) * LANES]
+            pieces = []
+            for k in range(nwidth // LANES):
+                thinned[slot, f, k] = x[:, k * LANES : (k + 1) * LANES]
+                a, b, c = [thinned[slot, f, k, pl.ds(i, tile, stride=3), :] for i in range(3)]
+                pieces.append(a + b + c)
+            lines.append(jnp.concatenate(pieces, axis=-1))
+        return lines
+
+    def pair(i, _):
+        group_of = [2 * i, 2 * i + 1]
+        for mem in group_of:
+            @pl.when(jnp.logical_not(first))
+            def _():
+                nest_down(mem, me).wait_recv()
+
+            @pl.when(jnp.logical_not(last))
+            def _():
+                nest_up(mem, me).wait_recv()
+
+        lines = [one_member(mem, slot) for slot, mem in enumerate(group_of)]
+        means = exact_dot(jnp.concatenate(lines[0] + lines[1], axis=0), thin) * (1.0 / 9.0)
+        for slot, mem in enumerate(group_of):
             for f in range(3):
-                parts = [thinned[k, pl.ds(f * nrows + i, tile, stride=3), :] for i in range(3)]
-                dealt[mem, k, f] = (parts[0] + parts[1] + parts[2]) * (1.0 / 9.0)
-        to = per * mem + turn_of
-
-        @pl.when(to != me)
-        def _():
-            mid_copy(mem, me, to).start()
-
-        @pl.when(to == me)
-        def _():
-            cbuf[:, :, pl.ds(pl.multiple_of(cpad + me * tile, tile), tile), :] = dealt[mem]
-
-        return 0
-
-    lax.fori_loop(0, members, one_member, 0)
+                at = (3 * slot + f) * tile
+                for k in range(span // LANES):
+                    dealt[mem, k, f] = means[at : at + tile, k * LANES : (k + 1) * LANES]
+            to = per * mem + turn_of
+
+            @pl.when(to != me)
+            def _():
+                mid_copy(mem, me, to).start()
+
+            @pl.when(to == me)
+            def _():
+                cbuf[:, :, pl.ds(pl.multiple_of(cpad + me * tile, tile), tile), :] = dealt[mem]
+
+        return 0
+
+    lax.fori_loop(0, members // 2, pair, 0)
     is_mid = lax.rem(me, per) == turn_of
     mine = me // per
 
@@ -418,7 +434,7 @@
             return 0
 
         lax.fori_loop(1, bands, recv, 0)
-        start_row = off_ref[mine, 0]
+        start_row = off_ref[0, mine]
 
         def deal(j, _):
             to = lax.rem(me + j, bands)
@@ -494,41 +510,29 @@
         lax.fori_loop(1, bands, sent_out, 0)
 
 
-def parent_kernel(span, bands, off_ref, band_ref, par_ref, halo_ref, patch_ref, out_ref):
+def parent_kernel(span, bands, off_ref, band_ref, par_ref, halo_ref, patch_ref, nest_ref, out_ref, nest_out):
+    nest_out[...] = nest_ref[...]
     mem = pl.program_id(0)
     rows, width = par_ref.shape[2], par_ref.shape[3]
-    row0, col0 = off_ref[mem, 0], off_ref[mem, 1]
+    row0, col0 = off_ref[0, mem], off_ref[1, mem]
     band = band_ref[0]
     first, last = band == 0, band == bands - 1
-    piece = 4 * LANES
-    row = iota((rows, piece + 2 * LANES), 0)
-    at_top, at_bottom = row == 0, row == rows - 1
+    h, z, m = par_ref[0, 0], par_ref[0, 1], par_ref[0, 2]
+    row = iota(h.shape, 0)
 
     def ddy(x, above, below):
-        return jnp.where(at_bottom, below, row_roll(x, -1)) - jnp.where(at_top, above, row_roll(x, 1))
-
-    for begin in range(0, width, piece):
-
-        def cut(ref, *index):
-            left, right = (begin - LANES) % width, (begin + piece) % width
-            if left + piece + 2 * LANES == right + LANES:
-                return ref[(*index, slice(left, right + LANES))]
-            parts = (left, left + LANES), (begin, begin + piece), (right, right + LANES)
-            return jnp.concatenate([ref[(*index, slice(*part))] for part in parts], axis=-1)
-
-        every = slice(None)
-        h, z, m = [cut(par_ref, 0, f, every) for f in range(3)]
-        above = cut(halo_ref, 0, 0, every)
-        below = cut(halo_ref, 1, 0, every)
-        m_above = jnp.where(first, 0.0, above[0:1])
-        m_below = jnp.where(last, 0.0, below[0:1])
-        h_above = jnp.where(first, 0.0, above[1:2] - half * m[0:1])
-        h_below = jnp.where(last, 0.0, below[1:2] + half * m[rows - 1 : rows])
-        h1 = h - half * (lane_roll(z, -1) - lane_roll(z, 1) + ddy(m, m_above, m_below))
-        z1 = keep * z - half * (lane_roll(h1, -1) - lane_roll(h1, 1)) + rotation * m
-        m1 = keep * m - half * ddy(h1, h_above, h_below) - rotation * z
-        for f, x in enumerate((h1, z1, m1)):
-            out_ref[0, f, :, begin : begin + piece] = x[:, LANES : LANES + piece]
+        up = jnp.where(row == 0, above, row_roll(x, 1))
+        down = jnp.where(row == rows - 1, below, row_roll(x, -1))
+        return down - up
+
+    m_above = jnp.where(first, 0.0, halo_ref[0, 0, 0:1, :])
+    m_below = jnp.where(last, 0.0, halo_ref[1, 0, 0:1, :])
+    h_above = jnp.where(first, 0.0, halo_ref[0, 0, 1:2, :] - half * m[0:1])
+    h_below = jnp.where(last, 0.0, halo_ref[1, 0, 1:2, :] + half * m[rows - 1 : rows])
+    h1 = h - courant * dx(z) - half * ddy(m, m_above, m_below)
+    out_ref[0, 0] = h1
+    out_ref[0, 1] = keep * z - courant * dx(h1) + rotation * m
+    out_ref[0, 2] = keep * m - half * ddy(h1, h_above, h_below) - rotation * z
 
     block0 = col0 // LANES
     shift = col0 - block0 * LANES
@@ -548,8 +552,9 @@
     tile = nrows // 3
     f32 = jnp.float32
     band = lax.axis_index("band").reshape(1).astype(jnp.int32)
+    offsets = offsets.T
     shape = jax.ShapeDtypeStruct
-    limit = 48 * 1024 * 1024
+    limit = 60 * 1024 * 1024
     parent_spec = pl.BlockSpec((1, 3, prows, width), lambda i, *_: (i, 0, 0, 0))
     edge_spec = pl.BlockSpec((2, 1, 2, width), lambda i, *_: (0, i, 0, 0))
 
@@ -579,7 +584,7 @@
             pltpu.VMEM((3, members, nwidth), f32),
             pltpu.VMEM((3, members, span + LANES), f32),
             pltpu.VMEM((span + LANES, nwidth), jnp.bfloat16),
-            pltpu.VMEM((span // LANES, 3 * nrows, LANES), f32),
+            pltpu.VMEM((2, 3, nwidth // LANES, nrows, LANES), f32),
             pltpu.VMEM((members, span // LANES, 3, tile, LANES), f32),
             pltpu.VMEM((span // LANES, 3, bands * tile + 2 * prows, LANES), f32),
             pltpu.VMEM((bands, 3, prows, span), f32),
@@ -602,9 +607,10 @@
         name="nest",
     )(offsets, nest_state, parent_state)
 
-    parent_out = pl.pallas_call(
+    nest_spec = pl.BlockSpec((1, 3, nrows, nwidth), lambda i, *_: (i, 0, 0, 0))
+    return pl.pallas_call(
         functools.partial(parent_kernel, span, bands),
-        out_shape=shape(parent_state.shape, f32),
+        out_shape=(shape(parent_state.shape, f32), shape(nest_state.shape, f32)),
         grid_spec=pltpu.PrefetchScalarGridSpec(
             num_scalar_prefetch=2,
             grid=(members,),
@@ -612,13 +618,13 @@
                 parent_spec,
                 edge_spec,
                 pl.BlockSpec((1, 3, prows, span), lambda i, *_: (i, 0, 0, 0)),
+                nest_spec,
             ],
-            out_specs=parent_spec,
+            out_specs=(parent_spec, nest_spec),
         ),
         compiler_params=pltpu.CompilerParams(vmem_limit_bytes=limit),
         name="parent",
-    )(offsets, band, parent_state, halo, patch)
-    return (parent_out, nest_out)
+    )(offsets, band, parent_state, halo, patch, nest_out)
 
 
 def solution(mesh):

time: 60.5 us -> 53.7 us (0.89)
  Pallas kernels: 56.7 us -> 52.8 us
  local copies, waits for them, and re-layouts: 2.83 us -> 0 us
    pallas_call x1, Pallas kernels: 45.3 us -> 42.2 us  [per_device(): pl.pallas_call(functools.partial(nest_kernel, bands, span), out_shape=(sh...]
    unnamed x4 -> x0, local copies, waits for them, and re-layouts: 2.83 us -> none
    pallas_call x1, Pallas kernels: 11.4 us -> 10.6 us  [per_device(): pl.pallas_call(functools.partial(parent_kernel, span, bands), out_shape=(...]
where the time goes in v6:
time: 53.7 us; the launch traced here: 53.4 us
  Pallas kernels  52.8 us (98%)
  between operations  0.64 us (1%)
    pallas_call x1, Pallas kernels, per_device(): pl.pallas_call(functools.partial(nest_kernel, bands, span), out_shape=(sh...  42.2 us
    pallas_call x1, Pallas kernels, per_device(): pl.pallas_call(functools.partial(parent_kernel, span, bands), out_shape=(...  10.6 us

profile of v6, /device:TPU:0, one launch (start us, length us, event | category | flops | bytes accessed | tf_op | source)
XLA Modules:
  0.0 53.4 jit_solution(6889750091448587152)
XLA Ops:
  0.6 42.2 %nest.1 = (f32[8,3,24,384]{3,2,1,0:T(8,128)}, f32[8,3,16,128]{3,2,1,0:T(8,128)}, f32[2,8,2,4096]{3,2,1,0:T(2,128)}) custom-call(s32[2,8]{1,0:T(2,128)} %bitcast.2, f32[8,3,24,384]{3,2,1,0:T(8,128)} %nest_ref.1, f32[8,3,16,4096]{3,2,1,0:T(8,128)} %par_ref.1), custom_call_target="tpu_custom_call" | custom-call | tf_op jit(solution)/shard_map/nest/pallas_call | solution.py:565
  42.8 10.6 %parent.1 = (f32[8,3,16,4096]{3,2,1,0:T(8,128)}, f32[8,3,24,384]{3,2,1,0:T(8,128)}) custom-call(s32[2,8]{1,0:T(2,128)} %bitcast.3, s32[1]{0:T(128)} %bitcast.1.band_ref, f32[8,3,16,4096]{3,2,1,0:T(8,128)} %par_ref.1, f32[2,8,2,4096]{3,2,1,0:T(2,128)} %get-tuple-element.5.halo_ref, f32[8,3,16,128]{3,2,1,0:T(8,128)} %get-tuple-element.6.patch_ref, ...), custom_call_target="tpu_custom_call" | custom-call | tf_op jit(solution)/shard_map/parent/pallas_call | solution.py:611

commit v7 on v6

--- a/solution.py
+++ b/solution.py
@@ -117,6 +117,24 @@
     return total
 
 
+def inner_step(mem, ref, first, last):
+    rows = ref.shape[2]
+    h, z, m = ref[mem, 0], ref[mem, 1], ref[mem, 2]
+    row = iota(h.shape, 0)
+    h_above = jnp.where(first, 0.0, -half * m[0:1])
+    h_below = jnp.where(last, 0.0, half * m[rows - 1 : rows])
+
+    def ddy(x, above, below):
+        up = jnp.where(row == 0, above, row_roll(x, 1))
+        down = jnp.where(row == rows - 1, below, row_roll(x, -1))
+        return down - up
+
+    h1 = h - half * (lane_roll(z, -1) - lane_roll(z, 1) + ddy(m, 0.0, 0.0))
+    ref[mem, 0] = h1
+    ref[mem, 1] = keep * z - half * (lane_roll(h1, -1) - lane_roll(h1, 1)) + rotation * m
+    ref[mem, 2] = keep * m - half * ddy(h1, h_above, h_below) - rotation * z
+
+
 def nest_kernel(
     bands,
     span,
@@ -126,6 +144,7 @@
     nest_out,
     patch,
     halo,
+    stepped,
     par_ref,
     edge_ref,
     strip_ref,
@@ -156,6 +175,7 @@
     out_recv,
     local_sem,
     parent_sem,
+    step_sem,
 ):
     me = lax.axis_index("band")
     group = lax.axis_index("member")
@@ -249,20 +269,6 @@
     @pl.when(sends_bottom)
     def _():
         end_copy(1, bands - 1 - me, bands - 1).start()
-
-    def send_edges(mem, _):
-        edge_rows(mem, par_ref, edge_ref)
-        return 0
-
-    lax.fori_loop(0, members, send_edges, 0)
-
-    @pl.when(jnp.logical_not(first))
-    def _():
-        edge_up(me - 1).start()
-
-    @pl.when(jnp.logical_not(last))
-    def _():
-        edge_down(me + 1).start()
 
     pad = strips.shape[0] - (bands + 1) * prows
     strips[pl.ds(0, prows), :] = jnp.zeros((prows, LANES), jnp.float32)
@@ -421,6 +427,11 @@
         return 0
 
     lax.fori_loop(0, members // 2, pair, 0)
+    def form_edges(mem, _):
+        edge_rows(mem, par_ref, edge_ref)
+        return 0
+
+    lax.fori_loop(0, members, form_edges, 0)
     is_mid = lax.rem(me, per) == turn_of
     mine = me // per
 
@@ -451,7 +462,28 @@
         lax.fori_loop(1, bands + 1, deal, 0)
         patch[mine] = sbuf[me]
 
+    @pl.when(jnp.logical_not(first))
+    def _():
+        edge_up(me - 1).start()
+
+    @pl.when(jnp.logical_not(last))
+    def _():
+        edge_down(me + 1).start()
+
+    def out_stepped(mem):
+        return pltpu.make_async_copy(par_ref.at[mem], stepped.at[mem], step_sem.at[mem])
+
+    def step_parent(mem, _):
+        inner_step(mem, par_ref, first, last)
+        out_stepped(mem).start()
+        return 0
+
+    lax.fori_loop(0, members, step_parent, 0)
+
     def recv_patch(mem, _):
+        out_stepped(mem).wait()
+
+
         @pl.when(per * mem + turn_of != me)
         def _():
             remote(sbuf.at[0], patch.at[mem], out_send.at[0], out_recv.at[mem], me).wait_recv()
@@ -513,26 +545,25 @@
 def parent_kernel(span, bands, off_ref, band_ref, par_ref, halo_ref, patch_ref, nest_ref, out_ref, nest_out):
     nest_out[...] = nest_ref[...]
     mem = pl.program_id(0)
-    rows, width = par_ref.shape[2], par_ref.shape[3]
+    rows = par_ref.shape[2]
     row0, col0 = off_ref[0, mem], off_ref[1, mem]
     band = band_ref[0]
-    first, last = band == 0, band == bands - 1
-    h, z, m = par_ref[0, 0], par_ref[0, 1], par_ref[0, 2]
-    row = iota(h.shape, 0)
-
-    def ddy(x, above, below):
-        up = jnp.where(row == 0, above, row_roll(x, 1))
-        down = jnp.where(row == rows - 1, below, row_roll(x, -1))
-        return down - up
-
-    m_above = jnp.where(first, 0.0, halo_ref[0, 0, 0:1, :])
-    m_below = jnp.where(last, 0.0, halo_ref[1, 0, 0:1, :])
-    h_above = jnp.where(first, 0.0, halo_ref[0, 0, 1:2, :] - half * m[0:1])
-    h_below = jnp.where(last, 0.0, halo_ref[1, 0, 1:2, :] + half * m[rows - 1 : rows])
-    h1 = h - courant * dx(z) - half * ddy(m, m_above, m_below)
-    out_ref[0, 0] = h1
-    out_ref[0, 1] = keep * z - courant * dx(h1) + rotation * m
-    out_ref[0, 2] = keep * m - half * ddy(h1, h_above, h_below) - rotation * z
+    out_ref[...] = par_ref[...]
+
+    def add(first_row, second_row, sign, halo):
+        m, p = half * halo[0:1], half * halo[1:2]
+        out_ref[0, 0, first_row : first_row + 1, :] += sign * m
+        out_ref[0, 1, first_row : first_row + 1, :] -= sign * half * (lane_roll(m, -1) - lane_roll(m, 1))
+        out_ref[0, 2, first_row : first_row + 1, :] += sign * p
+        out_ref[0, 2, second_row : second_row + 1, :] += half * m
+
+    @pl.when(band > 0)
+    def _():
+        add(0, 1, 1.0, halo_ref[0, 0])
+
+    @pl.when(band < bands - 1)
+    def _():
+        add(rows - 1, rows - 2, -1.0, halo_ref[1, 0])
 
     block0 = col0 // LANES
     shift = col0 - block0 * LANES
@@ -562,15 +593,16 @@
     hbm = pl.BlockSpec(memory_space=pl.ANY)
     dma = pltpu.SemaphoreType.DMA
     senders = bands // 2 + 1
-    nest_out, patch, halo = pl.pallas_call(
+    nest_out, patch, halo, stepped = pl.pallas_call(
         functools.partial(nest_kernel, bands, span),
         out_shape=(
             shape(nest_state.shape, f32),
             shape((members, 3, prows, span), f32),
             shape((2, members, 2, width), f32),
+            shape(parent_state.shape, f32),
         ),
         in_specs=[pl.BlockSpec(memory_space=pltpu.SMEM), hbm, hbm],
-        out_specs=(vmem, vmem, hbm),
+        out_specs=(vmem, vmem, hbm, hbm),
         scratch_shapes=[
             pltpu.VMEM((members, 3, prows, width), f32),
             pltpu.VMEM((2, members, 2, width), f32),
@@ -602,6 +634,7 @@
             dma((members,)),
             dma,
             dma,
+            dma((members,)),
         ],
         compiler_params=pltpu.CompilerParams(collective_id=0, has_side_effects=True, vmem_limit_bytes=limit),
         name="nest",
@@ -624,7 +657,7 @@
         ),
         compiler_params=pltpu.CompilerParams(vmem_limit_bytes=limit),
         name="parent",
-    )(offsets, band, parent_state, halo, patch, nest_out)
+    )(offsets, band, stepped, halo, patch, nest_out)
 
 
 def solution(mesh):

time: 53.7 us -> 53.7 us (level); the launches traced: 53.4 us -> 52.6 us
  Pallas kernels: 52.8 us -> 52 us
    pallas_call x1, Pallas kernels: 10.6 us -> 9.69 us  [per_device(): pl.pallas_call(functools.partial(parent_kernel, span, bands), out_shape=(...]
where the time goes in v7:
time: 53.7 us; the launch traced here: 52.6 us
  Pallas kernels  52 us (97%)
  between operations  0.64 us (1%)
    pallas_call x1, Pallas kernels, per_device(): pl.pallas_call(functools.partial(nest_kernel, bands, span), out_shape=(sh...  42.3 us
    pallas_call x1, Pallas kernels, per_device(): pl.pallas_call(functools.partial(parent_kernel, span, bands), out_shape=(...  9.69 us

profile of v7, /device:TPU:0, one launch (start us, length us, event | category | flops | bytes accessed | tf_op | source)
XLA Modules:
  0.0 52.6 jit_solution(11858658753887433471)
XLA Ops:
  0.6 42.3 %nest.1 = (f32[8,3,24,384]{3,2,1,0:T(8,128)}, f32[8,3,16,128]{3,2,1,0:T(8,128)}, f32[2,8,2,4096]{3,2,1,0:T(2,128)}, f32[8,3,16,4096]{3,2,1,0:T(8,128)}) custom-call(s32[2,8]{1,0:T(2,128)} %bitcast.2, f32[8,3,24,384]{3,2,1,0:T(8,128)} %nest_ref.1, f32[8,3,16,4096]{3,2,1,0:T(8,128)} %parent_ref.1), custom_call_target="tpu_custom_call" | custom-call | tf_op jit(solution)/shard_map/nest/pallas_call | solution.py:596
  42.9 9.7 %parent.1 = (f32[8,3,16,4096]{3,2,1,0:T(8,128)}, f32[8,3,24,384]{3,2,1,0:T(8,128)}) custom-call(s32[2,8]{1,0:T(2,128)} %bitcast.3, s32[1]{0:T(128)} %bitcast.1.band_ref, f32[8,3,16,4096]{3,2,1,0:T(8,128)} %get-tuple-element.6.par_ref, f32[2,8,2,4096]{3,2,1,0:T(2,128)} %get-tuple-element.7.halo_ref, f32[8,3,16,128]{3,2,1,0:T(8,128)} %get-tuple-element.8.patch_ref, ...), custom_call_target="tpu_custom_call" | custom-call | tf_op jit(solution)/shard_map/parent/pallas_call | solution.py:644

commit v8 on v7

--- a/solution.py
+++ b/solution.py
@@ -198,8 +198,12 @@
 
     lax.fori_loop(1, bands, greet, 0)
     own = pltpu.make_async_copy(nest_ref, ext.at[:, :, pl.ds(HALO, nrows), :], local_sem)
-    load = pltpu.make_async_copy(parent_ref, par_ref, parent_sem)
-    load.start()
+
+    def load(mem):
+        return pltpu.make_async_copy(parent_ref.at[mem], par_ref.at[mem], parent_sem.at[mem])
+
+    for mem in range(members):
+        load(mem).start()
     own.start()
     pl.semaphore_wait(barrier, bands - 1)
 
@@ -238,6 +242,8 @@
     first, last = me == 0, me == bands - 1
 
     def gather(mem, _):
+        load(mem).wait()
+
         @pl.when(jnp.logical_not(first))
         def _():
             nest_up(mem, me - 1).start()
@@ -250,7 +256,6 @@
         return 0
 
     strip_ref[...] = jnp.zeros_like(strip_ref)
-    load.wait()
     lax.fori_loop(0, members, gather, 0)
 
     def send_strip(j, _):
@@ -542,38 +547,96 @@
         lax.fori_loop(1, bands, sent_out, 0)
 
 
-def parent_kernel(span, bands, off_ref, band_ref, par_ref, halo_ref, patch_ref, nest_ref, out_ref, nest_out):
-    nest_out[...] = nest_ref[...]
-    mem = pl.program_id(0)
-    rows = par_ref.shape[2]
+def finish(mem, span, bands, off_ref, band_ref, halo_ref, patch_ref, out_ref):
+    rows = out_ref.shape[2]
     row0, col0 = off_ref[0, mem], off_ref[1, mem]
     band = band_ref[0]
-    out_ref[...] = par_ref[...]
 
     def add(first_row, second_row, sign, halo):
         m, p = half * halo[0:1], half * halo[1:2]
-        out_ref[0, 0, first_row : first_row + 1, :] += sign * m
-        out_ref[0, 1, first_row : first_row + 1, :] -= sign * half * (lane_roll(m, -1) - lane_roll(m, 1))
-        out_ref[0, 2, first_row : first_row + 1, :] += sign * p
-        out_ref[0, 2, second_row : second_row + 1, :] += half * m
+        out_ref[mem, 0, first_row : first_row + 1, :] += sign * m
+        out_ref[mem, 1, first_row : first_row + 1, :] -= sign * half * (lane_roll(m, -1) - lane_roll(m, 1))
+        out_ref[mem, 2, first_row : first_row + 1, :] += sign * p
+        out_ref[mem, 2, second_row : second_row + 1, :] += half * m
 
     @pl.when(band > 0)
     def _():
-        add(0, 1, 1.0, halo_ref[0, 0])
+        add(0, 1, 1.0, halo_ref[0, mem])
 
     @pl.when(band < bands - 1)
     def _():
-        add(rows - 1, rows - 2, -1.0, halo_ref[1, 0])
+        add(rows - 1, rows - 2, -1.0, halo_ref[1, mem])
 
     block0 = col0 // LANES
     shift = col0 - block0 * LANES
     place = pl.ds(pl.multiple_of(block0 * LANES, LANES), span + LANES)
-    wide = jnp.concatenate([patch_ref[0], jnp.zeros((3, rows, LANES), jnp.float32)], axis=-1)
+    wide = jnp.concatenate([patch_ref[mem], jnp.zeros((3, rows, LANES), jnp.float32)], axis=-1)
     wide = pltpu.roll(wide.reshape(3 * rows, span + LANES), shift, 1).reshape(3, rows, span + LANES)
     lane = iota(wide.shape, 2)
     at = iota(wide.shape, 1) + (band * rows - row0)
     inside = (lane >= shift) & (lane < shift + span) & (at >= 0) & (at < span)
-    out_ref[0, :, :, place] = jnp.where(inside, wide, out_ref[0, :, :, place])
+    out_ref[mem, :, :, place] = jnp.where(inside, wide, out_ref[mem, :, :, place])
+
+
+def parent_kernel(
+    span,
+    bands,
+    off_ref,
+    band_ref,
+    par_ref,
+    halo_ref,
+    patch_ref,
+    nest_ref,
+    out_ref,
+    nest_out,
+    work,
+    halos,
+    nests,
+    in_sem,
+    out_sem,
+    halo_sem,
+    nest_in,
+    nest_back,
+):
+    members = work.shape[0]
+
+    def move_halo(mem):
+        return pltpu.make_async_copy(halo_ref.at[:, mem], halos.at[:, mem], halo_sem.at[mem])
+
+    def move_in(mem):
+        return pltpu.make_async_copy(par_ref.at[mem], work.at[mem], in_sem.at[mem])
+
+    def move_out(mem):
+        return pltpu.make_async_copy(work.at[mem], out_ref.at[mem], out_sem.at[mem])
+
+    def nest_to(mem):
+        return pltpu.make_async_copy(nest_ref.at[mem], nests.at[mem], nest_in.at[mem])
+
+    def nest_from(mem):
+        return pltpu.make_async_copy(nests.at[mem], nest_out.at[mem], nest_back.at[mem])
+
+    for mem in range(members):
+        move_halo(mem).start()
+        move_in(mem).start()
+        nest_to(mem).start()
+
+    def one_member(mem, _):
+        move_halo(mem).wait()
+        move_in(mem).wait()
+        finish(mem, span, bands, off_ref, band_ref, halos, patch_ref, work)
+        move_out(mem).start()
+        nest_to(mem).wait()
+        nest_from(mem).start()
+        return 0
+
+    lax.fori_loop(0, members, one_member, 0)
+
+    def last_wait(mem, _):
+        move_out(mem).wait()
+        nest_from(mem).wait()
+        return 0
+
+    lax.fori_loop(0, members, last_wait, 0)
 
 
 def per_device(bands, parent_state, nest_state, offsets):
@@ -586,9 +649,6 @@
     offsets = offsets.T
     shape = jax.ShapeDtypeStruct
     limit = 60 * 1024 * 1024
-    parent_spec = pl.BlockSpec((1, 3, prows, width), lambda i, *_: (i, 0, 0, 0))
-    edge_spec = pl.BlockSpec((2, 1, 2, width), lambda i, *_: (0, i, 0, 0))
-
     vmem = pl.BlockSpec(memory_space=pltpu.VMEM)
     hbm = pl.BlockSpec(memory_space=pl.ANY)
     dma = pltpu.SemaphoreType.DMA
@@ -633,28 +693,29 @@
             dma((bands,)),
             dma((members,)),
             dma,
-            dma,
+            dma((members,)),
             dma((members,)),
         ],
         compiler_params=pltpu.CompilerParams(collective_id=0, has_side_effects=True, vmem_limit_bytes=limit),
         name="nest",
     )(offsets, nest_state, parent_state)
 
-    nest_spec = pl.BlockSpec((1, 3, nrows, nwidth), lambda i, *_: (i, 0, 0, 0))
+    smem = pl.BlockSpec(memory_space=pltpu.SMEM)
     return pl.pallas_call(
         functools.partial(parent_kernel, span, bands),
         out_shape=(shape(parent_state.shape, f32), shape(nest_state.shape, f32)),
-        grid_spec=pltpu.PrefetchScalarGridSpec(
-            num_scalar_prefetch=2,
-            grid=(members,),
-            in_specs=[
-                parent_spec,
-                edge_spec,
-                pl.BlockSpec((1, 3, prows, span), lambda i, *_: (i, 0, 0, 0)),
-                nest_spec,
-            ],
-            out_specs=(parent_spec, nest_spec),
-        ),
+        in_specs=[smem, smem, hbm, hbm, vmem, hbm],
+        out_specs=(hbm, hbm),
+        scratch_shapes=[
+            pltpu.VMEM((members, 3, prows, width), f32),
+            pltpu.VMEM((2, members, 2, width), f32),
+            pltpu.VMEM((members, 3, nrows, nwidth), f32),
+            dma((members,)),
+            dma((members,)),
+            dma((members,)),
+            dma((members,)),
+            dma((members,)),
+        ],
         compiler_params=pltpu.CompilerParams(vmem_limit_bytes=limit),
         name="parent",
     )(offsets, band, stepped, halo, patch, nest_out)

time: 53.7 us -> 50.7 us (0.944)
  Pallas kernels: 52 us -> 49.4 us
    pallas_call x1, Pallas kernels: 9.69 us -> 7.52 us  [per_device(): pl.pallas_call(functools.partial(parent_kernel, span, bands), out_shape=(...]
where the time goes in v8:
time: 50.7 us; the launch traced here: 50.1 us
  Pallas kernels  49.4 us (97%)
  between operations  0.64 us (1%)
    pallas_call x1, Pallas kernels, per_device(): pl.pallas_call(functools.partial(nest_kernel, bands, span), out_shape=(sh...  41.9 us
    pallas_call x1, Pallas kernels, per_device(): pl.pallas_call(functools.partial(parent_kernel, span, bands), out_shape=(...  7.52 us

profile of v8, /device:TPU:0, one launch (start us, length us, event | category | flops | bytes accessed | tf_op | source)
XLA Modules:
  0.0 50.1 jit_solution(14999419604435495838)
XLA Ops:
  0.6 41.9 %nest.1 = (f32[8,3,24,384]{3,2,1,0:T(8,128)}, f32[8,3,16,128]{3,2,1,0:T(8,128)}, f32[2,8,2,4096]{3,2,1,0:T(2,128)}, f32[8,3,16,4096]{3,2,1,0:T(8,128)}) custom-call(s32[2,8]{1,0:T(2,128)} %bitcast.2, f32[8,3,24,384]{3,2,1,0:T(8,128)} %nest_ref.1, f32[8,3,16,4096]{3,2,1,0:T(8,128)} %parent_ref.1), custom_call_target="tpu_custom_call" | custom-call | tf_op jit(solution)/shard_map/nest/pallas_call | solution.py:656
  42.5 7.5 %parent.1 = (f32[8,3,16,4096]{3,2,1,0:T(8,128)}, f32[8,3,24,384]{3,2,1,0:T(8,128)}) custom-call(s32[2,8]{1,0:T(2,128)} %bitcast.3, s32[1]{0:T(128)} %bitcast.1.band_ref, f32[8,3,16,4096]{3,2,1,0:T(8,128)} %get-tuple-element.6.par_ref, f32[2,8,2,4096]{3,2,1,0:T(2,128)} %get-tuple-element.7.halo_ref, f32[8,3,16,128]{3,2,1,0:T(8,128)} %get-tuple-element.8.patch_ref, ...), custom_call_target="tpu_custom_call" | custom-call | tf_op jit(solution)/shard_map/parent/pallas_call | solution.py:704

commit v9 on v8

--- a/solution.py
+++ b/solution.py
@@ -275,6 +275,20 @@
     def _():
         end_copy(1, bands - 1 - me, bands - 1).start()
 
+    def form_edges(mem, _):
+        edge_rows(mem, par_ref, edge_ref)
+        return 0
+
+    lax.fori_loop(0, members, form_edges, 0)
+
+    @pl.when(jnp.logical_not(first))
+    def _():
+        edge_up(me - 1).start()
+
+    @pl.when(jnp.logical_not(last))
+    def _():
+        edge_down(me + 1).start()
+
     pad = strips.shape[0] - (bands + 1) * prows
     strips[pl.ds(0, prows), :] = jnp.zeros((prows, LANES), jnp.float32)
     strips[pl.ds((bands + 1) * prows, pad), :] = jnp.zeros((pad, LANES), jnp.float32)
@@ -432,11 +446,6 @@
         return 0
 
     lax.fori_loop(0, members // 2, pair, 0)
-    def form_edges(mem, _):
-        edge_rows(mem, par_ref, edge_ref)
-        return 0
-
-    lax.fori_loop(0, members, form_edges, 0)
     is_mid = lax.rem(me, per) == turn_of
     mine = me // per
 
@@ -466,14 +475,6 @@
 
         lax.fori_loop(1, bands + 1, deal, 0)
         patch[mine] = sbuf[me]
-
-    @pl.when(jnp.logical_not(first))
-    def _():
-        edge_up(me - 1).start()
-
-    @pl.when(jnp.logical_not(last))
-    def _():
-        edge_down(me + 1).start()
 
     def out_stepped(mem):
         return pltpu.make_async_copy(par_ref.at[mem], stepped.at[mem], step_sem.at[mem])

time: 50.7 us -> 51.2 us (level)
  Pallas kernels: 49.4 us -> 50.3 us
    pallas_call x1, Pallas kernels: 41.9 us -> 42.8 us  [per_device(): pl.pallas_call(functools.partial(nest_kernel, bands, span), out_shape=(sh...]
where the time goes in v9:
time: 51.2 us; the launch traced here: 51 us
  Pallas kernels  50.3 us (98%)
  between operations  0.64 us (1%)
    pallas_call x1, Pallas kernels, per_device(): pl.pallas_call(functools.partial(nest_kernel, bands, span), out_shape=(sh...  42.8 us
    pallas_call x1, Pallas kernels, per_device(): pl.pallas_call(functools.partial(parent_kernel, span, bands), out_shape=(...  7.52 us

profile of v9, /device:TPU:0, one launch (start us, length us, event | category | flops | bytes accessed | tf_op | source)
XLA Modules:
  0.0 51.0 jit_solution(8410351985210611647)
XLA Ops:
  0.6 42.8 %nest.1 = (f32[8,3,24,384]{3,2,1,0:T(8,128)}, f32[8,3,16,128]{3,2,1,0:T(8,128)}, f32[2,8,2,4096]{3,2,1,0:T(2,128)}, f32[8,3,16,4096]{3,2,1,0:T(8,128)}) custom-call(s32[2,8]{1,0:T(2,128)} %bitcast.2, f32[8,3,24,384]{3,2,1,0:T(8,128)} %nest_ref.1, f32[8,3,16,4096]{3,2,1,0:T(8,128)} %parent_ref.1), custom_call_target="tpu_custom_call" | custom-call | tf_op jit(solution)/shard_map/nest/pallas_call | solution.py:657
  43.5 7.5 %parent.1 = (f32[8,3,16,4096]{3,2,1,0:T(8,128)}, f32[8,3,24,384]{3,2,1,0:T(8,128)}) custom-call(s32[2,8]{1,0:T(2,128)} %bitcast.3, s32[1]{0:T(128)} %bitcast.1.band_ref, f32[8,3,16,4096]{3,2,1,0:T(8,128)} %get-tuple-element.6.par_ref, f32[2,8,2,4096]{3,2,1,0:T(2,128)} %get-tuple-element.7.halo_ref, f32[8,3,16,128]{3,2,1,0:T(8,128)} %get-tuple-element.8.patch_ref, ...), custom_call_target="tpu_custom_call" | custom-call | tf_op jit(solution)/shard_map/parent/pallas_call | solution.py:705
